TPU v7x, 32 devices: a whole 2x2x4 slice. The times are simulated.
32 devices in a mesh: seq: 8 (over z, y), head: 4 (over x, core).
Axes of the slice: x: 2, y: 2, z: 4, core: 2. Of those that a mesh axis runs over, the one named last changes fastest.
Arguments:
- queries: bfloat16 [8192, 3072], P('seq', 'head'), may hold values from -10 to 10
- keys: bfloat16 [8192, 3072], P('seq', 'head'), may hold values from -4 to 4
- values: bfloat16 [8192, 3072], P('seq', 'head'), may hold values from -4 to 4
- w_out: bfloat16 [3072, 3072], P('head', 'seq'), may hold values from -0.21875 to 0.21875
- head_kind: int32 [24], replicated, may hold values from 0 to 1, as said below
- band_offsets: int32 [2, 7], replicated, may hold values from -4 to 4, as said below
Outputs:
- mixed: bfloat16 [8192, 3072], P(('seq', 'head'))
Inputs may be any that keep to these rules, and one draw needn't show every extreme that they name: `head_kind`: each group of 6 consecutive heads holds at most 5 temporal heads, and some group holds exactly that many. `band_offsets`: each row holds 7 distinct offsets and always contains 0, 4 and minus 4.
All inputs are finite; a program needn't handle non-finite values.
Results may differ from a plain program's by a relative error of at most 0.013.
Values may be sent and summed in bfloat16 or wider, within the bound.
No kernel may reach another device: no remote copies, remote signals or barrier semaphores. Data moves between devices by JAX's collectives and lax.ppermute only.
A program may use at most 128 MiB of HBM per device.

v0:
```python
import math

import jax
import jax.numpy as jnp
from jax import lax
from jax.sharding import PartitionSpec as P

DH = 128
FRAMES = 16
BLK = 256


def with_halo(cells, sides, width):
    for axis, dim in sides:
        count = lax.axis_size(axis)
        ends = count - 1
        head = lax.slice_in_dim(cells, 0, width, axis=dim)
        tail = lax.slice_in_dim(cells, cells.shape[dim] - width, cells.shape[dim], axis=dim)
        cells = jnp.concatenate(
            [
                lax.ppermute(tail, axis, [(i, (i + 1) % count) for i in range(ends)]),
                cells,
                lax.ppermute(head, axis, [((i + 1) % count, i) for i in range(ends)]),
            ],
            axis=dim,
        )
    return cells


def split_shape(field_rows, seq_count):
    tok_dev, channels = field_rows.shape
    positions = tok_dev * seq_count // FRAMES
    span_rows = min(tok_dev, positions)
    return field_rows.reshape(tok_dev // span_rows, seq_count, span_rows // seq_count, channels)


def temporal_order(moved_rows):
    channels = moved_rows.shape[3]
    quota_rows = moved_rows.shape[2]
    halves = moved_rows.shape[0] // FRAMES
    grid_view = moved_rows.reshape(FRAMES, halves, quota_rows, channels)
    return grid_view.transpose(1, 2, 0, 3).reshape(halves * quota_rows * FRAMES, channels)


def frame_order(field_rows, seq_count):
    tok_dev, channels = field_rows.shape
    positions = tok_dev * seq_count // FRAMES
    span_rows = min(tok_dev, positions)
    quota_rows = span_rows // seq_count
    halves = positions // span_rows
    grid_view = field_rows.reshape(halves, quota_rows, FRAMES, channels)
    return grid_view.transpose(2, 0, 1, 3).reshape(FRAMES * halves, 1, quota_rows, channels)


def band_attend(query_rows, key_ext, value_ext, offsets, first_block, total_blocks):
    local_blocks = query_rows.shape[0] // BLK
    head_size = query_rows.shape[1]
    offset_count = offsets.shape[0]
    query_blocks = query_rows.reshape(local_blocks, BLK, head_size)
    k_blocks = key_ext.reshape(3 * local_blocks, BLK, head_size)
    v_blocks = value_ext.reshape(3 * local_blocks, BLK, head_size)
    target = jnp.arange(local_blocks, dtype=jnp.int32)[:, None] + offsets[None, :]
    global_block = first_block + target
    in_range = (global_block >= 0) & (global_block < total_blocks)
    key_index = jnp.clip(target + local_blocks, 0, 3 * local_blocks - 1)
    nearby_keys = jnp.take(k_blocks, key_index, axis=0).reshape(
        local_blocks, offset_count * BLK, head_size
    )
    nearby_values = jnp.take(v_blocks, key_index, axis=0).reshape(
        local_blocks, offset_count * BLK, head_size
    )
    score_scale = 1.0 / math.sqrt(head_size)
    attention_scores = (
        jnp.einsum("vuf,vzf->vuz", query_blocks, nearby_keys, preferred_element_type=jnp.float32)
        * score_scale
    )
    allowed = jnp.broadcast_to(in_range[:, :, None], (local_blocks, offset_count, BLK))
    allowed = allowed.reshape(local_blocks, 1, offset_count * BLK)
    attention_scores = jnp.where(allowed, attention_scores, -1e30)
    row_max = jnp.max(attention_scores, axis=2, keepdims=True)
    weights = jnp.exp(attention_scores - row_max)
    attention_probabilities = (weights / jnp.sum(weights, axis=2, keepdims=True)).astype(
        jnp.bfloat16
    )
    attended_output = jnp.einsum(
        "oyx,oxi->oyi", attention_probabilities, nearby_values, preferred_element_type=jnp.float32
    )
    return attended_output.astype(jnp.bfloat16).reshape(local_blocks * BLK, head_size)


def body(queries, keys, values, w_out, head_kind, band_offsets):
    seq_count = lax.axis_size("seq")
    seq_rank = lax.axis_index("seq")
    head_rank = lax.axis_index("head")
    tok_dev = queries.shape[0]
    head_dev = queries.shape[1] // DH
    head_types = lax.dynamic_slice_in_dim(head_kind, head_rank * head_dev, head_dev)
    is_temporal = head_types == 1
    query_heads = queries.reshape(tok_dev, head_dev, DH)
    key_heads = keys.reshape(tok_dev, head_dev, DH)
    value_heads = values.reshape(tok_dev, head_dev, DH)
    select_mask = is_temporal[None, :, None]
    moved_q, moved_k, moved_v = (
        lax.all_to_all(
            split_shape(queries, seq_count), "seq", split_axis=1, concat_axis=0, tiled=True
        ),
        lax.all_to_all(
            split_shape(keys, seq_count), "seq", split_axis=1, concat_axis=0, tiled=True
        ),
        lax.all_to_all(
            split_shape(values, seq_count), "seq", split_axis=1, concat_axis=0, tiled=True
        ),
    )
    relaid_q = temporal_order(moved_q).reshape(tok_dev, head_dev, DH)
    relaid_k = temporal_order(moved_k).reshape(tok_dev, head_dev, DH)
    relaid_v = temporal_order(moved_v).reshape(tok_dev, head_dev, DH)
    chosen_q = jnp.where(select_mask, relaid_q, query_heads)
    chosen_k = jnp.where(select_mask, relaid_k, key_heads)
    chosen_v = jnp.where(select_mask, relaid_v, value_heads)
    pair_rows = jnp.concatenate(
        [chosen_k.reshape(tok_dev, head_dev * DH), chosen_v.reshape(tok_dev, head_dev * DH)], axis=1
    )
    extended = with_halo(pair_rows, (("seq", 0),), tok_dev)
    key_ext = extended[:, : head_dev * DH].reshape(3 * tok_dev, head_dev, DH).transpose(1, 0, 2)
    value_ext = extended[:, head_dev * DH :].reshape(3 * tok_dev, head_dev, DH).transpose(1, 0, 2)
    head_offsets = jnp.where(
        is_temporal[:, None], band_offsets[1][None, :], band_offsets[0][None, :]
    )
    local_blocks = tok_dev // BLK
    first_block = seq_rank * local_blocks
    total_blocks = local_blocks * seq_count

    def attend_head(head_items):
        return band_attend(
            head_items[0], head_items[1], head_items[2], head_items[3], first_block, total_blocks
        )

    per_head = lax.map(attend_head, (chosen_q.transpose(1, 0, 2), key_ext, value_ext, head_offsets))
    attended_output = per_head.transpose(1, 0, 2)
    returned = lax.all_to_all(
        frame_order(attended_output.reshape(tok_dev, head_dev * DH), seq_count),
        "seq",
        split_axis=0,
        concat_axis=1,
        tiled=True,
    )
    returned = returned.reshape(tok_dev, head_dev, DH)
    final_rows = jnp.where(select_mask, returned, attended_output).reshape(tok_dev, head_dev * DH)
    weight_rows = lax.all_gather(w_out, "seq", axis=1, tiled=True)
    group_count = lax.axis_size("head")
    every_row = lax.all_gather(weight_rows, "head", axis=0, tiled=True)
    token_rows = lax.all_to_all(final_rows, "head", split_axis=0, concat_axis=1, tiled=True)
    own_rows = token_rows.shape[0]
    grouped = jnp.einsum(
        "rgc,gcd->grd",
        token_rows.reshape(own_rows, group_count, head_dev * DH),
        every_row.reshape(group_count, head_dev * DH, every_row.shape[1]),
        preferred_element_type=jnp.float32,
    ).astype(jnp.bfloat16)
    grouped = lax.optimization_barrier(grouped)
    return jnp.sum(grouped.astype(jnp.float32), axis=0).astype(jnp.bfloat16)


def solution(mesh):
    return jax.shard_map(
        body,
        mesh=mesh,
        in_specs=(P("seq", "head"), P("seq", "head"), P("seq", "head"), P("head", "seq"), P(), P()),
        out_specs=P(("seq", "head"), None),
        check_vma=False,
    )
```

profile of v0, /device:TPU:0, one launch (start us, length us, event | category | flops | bytes accessed | tf_op | source)
XLA Modules:
  0.0 586.1 jit_solution(16008286302888185157)
XLA Ops:
  9.2 7.4 %all-to-all-start.1 = ((bf16[2,8,64,768]{3,2,0,1:T(8,128)(2,1)}), bf16[2,8,64,768]{3,2,0,1:T(8,128)(2,1)S(1)}, u32[]{:S(2)}, u32[]{:S(2)}) async-start(bf16[2,8,64,768]{3,2,0,1:T(8,128)(2,1)} %copy.60), calls=%async_computation.1 | async-start | bytes 3145728 | tf_op jit(solution)/shard_map/all_to_all | solution.py:107
  18.6 54.0 %all-to-all-done.1 = bf16[2,8,64,768]{3,2,0,1:T(8,128)(2,1)S(1)} async-done(((bf16[2,8,64,768]{3,2,0,1:T(8,128)(2,1)}), bf16[2,8,64,768]{3,2,0,1:T(8,128)(2,1)S(1)}, u32[]{:S(2)}, u32[]{:S(2)}) %all-to-all-start.1) | async-done | bytes 1572896 | tf_op jit(solution)/shard_map/all_to_all | solution.py:107
  72.6 4.3 all-to-all-start.2
  79.1 67.5 %all-to-all-done.2 = bf16[2,8,64,768]{3,2,0,1:T(8,128)(2,1)} async-done(((bf16[2,8,64,768]{3,2,0,1:T(8,128)(2,1)}), bf16[2,8,64,768]{3,2,0,1:T(8,128)(2,1)}, u32[]{:S(2)}, u32[]{:S(2)}) %all-to-all-start.2) | async-done | bytes 1572896 | tf_op jit(solution)/shard_map/all_to_all | solution.py:110
  152.3 7.6 %collective-permute-start = (bf16[1024,1536]{1,0:T(8,128)(2,1)}, bf16[1024,1536]{1,0:T(8,128)(2,1)}, u32[]{:S(2)}, u32[]{:S(2)}) collective-permute-start(bf16[1024,1536]{1,0:T(8,128)(2,1)} %pad_maximum_fusion.1), channel_id=1, source_target_pairs={{0,4},{4,8},{8,12},{12,16},{16,20},{20,24},{24,28},{1,5},{5,9},{9,... | collective-permute-start | bytes 9437192 | tf_op jit(solution)/shard_map/ppermute | solution.py:21
  162.4 5.1 all-to-all-start
  173.3 135.9 %all-to-all-done = bf16[2,8,64,768]{3,2,0,1:T(8,128)(2,1)} async-done(((bf16[2,8,64,768]{3,2,0,1:T(8,128)(2,1)}), bf16[2,8,64,768]{3,2,0,1:T(8,128)(2,1)}, u32[]{:S(2)}, u32[]{:S(2)}) %all-to-all-start) | async-done | bytes 1572896 | tf_op jit(solution)/shard_map/all_to_all | solution.py:104
  312.6 4.3 reshape_reshape.12
  321.3 4.5 pad_maximum_fusion
  325.8 4.3 fusion.18
  330.1 6.6 %copy.64 = bf16[3072,768]{0,1:T(8,128)(2,1)} copy(bf16[3072,768]{1,0:T(8,128)(2,1)} %get-tuple-element.95) | data formatting | bytes 9437184 | tf_op jit(solution)/shard_map/slice | solution.py:124
  336.8 6.7 %copy.65 = bf16[3072,768]{0,1:T(8,128)(2,1)} copy(bf16[3072,768]{1,0:T(8,128)(2,1)} %get-tuple-element.94) | data formatting | bytes 9437184 | tf_op jit(solution)/shard_map/slice | solution.py:125
  343.5 132.5 %while.10 = (s32[]{:T(128)}, bf16[6,1024,128]{2,1,0:T(8,128)(2,1)}, s32[]{:T(128)}, s32[6,7]{1,0:T(8,128)S(1)}, bf16[6,1024,128]{2,1,0:T(8,128)(2,1)}, /*index=5...) while((s32[]{:T(128)}, bf16[6,1024,128]{2,1,0:T(8,128)(2,1)}, s32[]{:T(128)}, ...), condition=%wide.region_3.5_spmd, body=%wide.region_0.4_spmd.sunk | while | flops 952503552 | bytes 48276992 | solution.py:138
  353.6 7.0 %fusion.37 = (f32[4,256]{1,0:T(4,128)S(1)}, f32[4,256,1792]{2,1,0:T(8,128)}) fusion(pred[4,1792]{1,0:T(4,128)(4,1)S(1)} %bitcast.131, bf16[4,256,128]{2,1,0:T(8,128)(2,1)S(1)} %bitcast.121, bf16[4,1792,128]{2,1,0:T(8,128)(2,1)} %bitcast.117), kind=kOutput, calls=%fused_computation.47.clone.1 | convolution fusion | flops 477103872 | bytes 9448448 | tf_op jit(solution)/shard_map/while/body/eval_jaxpr/sub | solution.py:81
  375.7 7.0 %fusion.37 = (f32[4,256]{1,0:T(4,128)S(1)}, f32[4,256,1792]{2,1,0:T(8,128)}) fusion(pred[4,1792]{1,0:T(4,128)(4,1)S(1)} %bitcast.131, bf16[4,256,128]{2,1,0:T(8,128)(2,1)S(1)} %bitcast.121, bf16[4,1792,128]{2,1,0:T(8,128)(2,1)} %bitcast.117), kind=kOutput, calls=%fused_computation.47.clone.1 | convolution fusion | flops 477103872 | bytes 9448448 | tf_op jit(solution)/shard_map/while/body/eval_jaxpr/sub | solution.py:81
  382.7 4.3 fusion.38
  397.8 7.0 %fusion.37 = (f32[4,256]{1,0:T(4,128)S(1)}, f32[4,256,1792]{2,1,0:T(8,128)}) fusion(pred[4,1792]{1,0:T(4,128)(4,1)S(1)} %bitcast.131, bf16[4,256,128]{2,1,0:T(8,128)(2,1)S(1)} %bitcast.121, bf16[4,1792,128]{2,1,0:T(8,128)(2,1)} %bitcast.117), kind=kOutput, calls=%fused_computation.47.clone.1 | convolution fusion | flops 477103872 | bytes 9448448 | tf_op jit(solution)/shard_map/while/body/eval_jaxpr/sub | solution.py:81
  419.9 7.0 %fusion.37 = (f32[4,256]{1,0:T(4,128)S(1)}, f32[4,256,1792]{2,1,0:T(8,128)}) fusion(pred[4,1792]{1,0:T(4,128)(4,1)S(1)} %bitcast.131, bf16[4,256,128]{2,1,0:T(8,128)(2,1)S(1)} %bitcast.121, bf16[4,1792,128]{2,1,0:T(8,128)(2,1)} %bitcast.117), kind=kOutput, calls=%fused_computation.47.clone.1 | convolution fusion | flops 477103872 | bytes 9448448 | tf_op jit(solution)/shard_map/while/body/eval_jaxpr/sub | solution.py:81
  441.9 7.0 %fusion.37 = (f32[4,256]{1,0:T(4,128)S(1)}, f32[4,256,1792]{2,1,0:T(8,128)}) fusion(pred[4,1792]{1,0:T(4,128)(4,1)S(1)} %bitcast.131, bf16[4,256,128]{2,1,0:T(8,128)(2,1)S(1)} %bitcast.121, bf16[4,1792,128]{2,1,0:T(8,128)(2,1)} %bitcast.117), kind=kOutput, calls=%fused_computation.47.clone.1 | convolution fusion | flops 477103872 | bytes 9448448 | tf_op jit(solution)/shard_map/while/body/eval_jaxpr/sub | solution.py:81
  464.0 7.0 %fusion.37 = (f32[4,256]{1,0:T(4,128)S(1)}, f32[4,256,1792]{2,1,0:T(8,128)}) fusion(pred[4,1792]{1,0:T(4,128)(4,1)S(1)} %bitcast.131, bf16[4,256,128]{2,1,0:T(8,128)(2,1)S(1)} %bitcast.121, bf16[4,1792,128]{2,1,0:T(8,128)(2,1)} %bitcast.117), kind=kOutput, calls=%fused_computation.47.clone.1 | convolution fusion | flops 477103872 | bytes 9448448 | tf_op jit(solution)/shard_map/while/body/eval_jaxpr/sub | solution.py:81
  483.3 42.6 %all_to_all.85 = bf16[16,1,64,768]{3,2,1,0:T(8,128)(2,1)S(1)} all-to-all(bf16[16,1,64,768]{3,2,1,0:T(8,128)(2,1)S(1)} %copy.70), channel_id=1, replica_groups=mesh['seq'=8,'head'=4] {'seq'}, dimensions={0} | all-to-all | bytes 3145728 | tf_op jit(solution)/shard_map/all_to_all | solution.py:140
  537.8 22.6 %all_to_all.86 = bf16[4,256,768]{2,1,0:T(8,128)(2,1)S(1)} all-to-all(bf16[4,256,768]{2,1,0:T(8,128)(2,1)S(1)} %reshape.131), channel_id=1, replica_groups=mesh['seq'=8,'head'=4] {'head'}, dimensions={0} | all-to-all | bytes 3145728 | tf_op jit(solution)/shard_map/all_to_all | solution.py:152
  560.4 13.3 %convolution_convert_fusion = bf16[4,256,3072]{2,1,0:T(8,128)(2,1)} fusion(bf16[4,768,3072]{2,1,0:T(8,128)(2,1)} %bitcast.132, bf16[4,256,768]{2,1,0:T(8,128)(2,1)S(1)} %all_to_all.86), kind=kOutput, calls=%fused_computation.33 | convolution fusion | flops 4834983936 | bytes 26738688 | tf_op jit(solution)/shard_map/rgc,gcd->grd/dot_general | solution.py:154
  573.8 5.5 reduce_sum.21
  (160 shorter events, 133.8 us)
Async XLA Ops:
  9.2 8.2 %copy-start.6 = (bf16[1024,768]{1,0:T(8,128)(2,1)S(1)}, bf16[1024,768]{1,0:T(8,128)(2,1)}, u32[]{:S(2)}) copy-start(bf16[1024,768]{1,0:T(8,128)(2,1)} %param.12) | copy-start | bytes 4718596
  9.2 63.4 %all-to-all-start.1 = ((bf16[2,8,64,768]{3,2,0,1:T(8,128)(2,1)}), bf16[2,8,64,768]{3,2,0,1:T(8,128)(2,1)S(1)}, u32[]{:S(2)}, u32[]{:S(2)}) async-start(bf16[2,8,64,768]{3,2,0,1:T(8,128)(2,1)} %copy.60), calls=%async_computation.1 | async-start | bytes 3145728 | tf_op jit(solution)/shard_map/all_to_all | solution.py:107
  16.6 151.1 %all-gather.3.cloned.1.call-start = ((), (), s32[]{:S(2)}) async-start(), calls=%async_computation.5 | async-start | bytes 5308416 | tf_op jit(solution)/shard_map/all_gather | solution.py:149
  18.6 58.3 %copy-start.10 = (s32[24]{0:T(128)S(1)}, s32[24]{0:T(128)}, u32[]{:S(2)}) copy-start(s32[24]{0:T(128)} %param.14) | copy-start | bytes 292
  72.6 74.0 %all-to-all-start.2 = ((bf16[2,8,64,768]{3,2,0,1:T(8,128)(2,1)}), bf16[2,8,64,768]{3,2,0,1:T(8,128)(2,1)}, u32[]{:S(2)}, u32[]{:S(2)}) async-start(bf16[2,8,64,768]{3,2,0,1:T(8,128)(2,1)} %copy.62), calls=%async_computation.2 | async-start | bytes 3145728 | tf_op jit(solution)/shard_map/all_to_all | solution.py:110
  79.1 69.9 %copy-start.5 = (bf16[1024,768]{1,0:T(8,128)(2,1)S(1)}, bf16[1024,768]{1,0:T(8,128)(2,1)}, u32[]{:S(2)}) copy-start(bf16[1024,768]{1,0:T(8,128)(2,1)} %param.11) | copy-start | bytes 4718596
  146.6 2.4 copy-start.8
  149.5 2.2 copy-start.1
  149.5 2.7 copy-start.3
  149.5 11.6 %copy-start.7 = (bf16[1024,768]{1,0:T(8,128)(2,1)S(1)}, bf16[1024,768]{1,0:T(8,128)(2,1)}, u32[]{:S(2)}) copy-start(bf16[1024,768]{1,0:T(8,128)(2,1)} %param.10) | copy-start | bytes 4718596
  152.3 167.9 %collective-permute-start = (bf16[1024,1536]{1,0:T(8,128)(2,1)}, bf16[1024,1536]{1,0:T(8,128)(2,1)}, u32[]{:S(2)}, u32[]{:S(2)}) collective-permute-start(bf16[1024,1536]{1,0:T(8,128)(2,1)} %pad_maximum_fusion.1), channel_id=1, source_target_pairs={{0,4},{4,8},{8,12},{12,16},{16,20},{20,24},{24,28},{1,5},{5,9},{9,... | collective-permute-start | bytes 9437192 | tf_op jit(solution)/shard_map/ppermute | solution.py:21
  159.9 160.4 %collective-permute-start.1 = (bf16[1024,1536]{1,0:T(8,128)(2,1)}, bf16[1024,1536]{1,0:T(8,128)(2,1)}, u32[]{:S(2)}, u32[]{:S(2)}) collective-permute-start(bf16[1024,1536]{1,0:T(8,128)(2,1)} %pad_maximum_fusion.1), channel_id=1, source_target_pairs={{4,0},{8,4},{12,8},{16,12},{20,16},{24,20},{28,24},{5,1},{9,5},{13... | collective-permute-start | bytes 9437192 | tf_op jit(solution)/shard_map/ppermute | solution.py:23
  162.4 146.8 %all-to-all-start = ((bf16[2,8,64,768]{3,2,0,1:T(8,128)(2,1)}), bf16[2,8,64,768]{3,2,0,1:T(8,128)(2,1)}, u32[]{:S(2)}, u32[]{:S(2)}) async-start(bf16[2,8,64,768]{3,2,0,1:T(8,128)(2,1)} %copy.56), calls=%async_computation | async-start | bytes 3145728 | tf_op jit(solution)/shard_map/all_to_all | solution.py:104
  167.5 392.9 %all-gather.5.cloned.1.call-start = ((), (), s32[]{:S(2)}) async-start(), calls=%async_computation.6 | async-start | bytes 23592960 | tf_op jit(solution)/shard_map/all_gather | solution.py:151
  169.9 3.3 copy-start.9
  318.9 2.0 copy-start.2
  318.9 2.4 copy-start.4
  353.6 7.0 %copy-start = (bf16[4,7,256,128]{3,2,1,0:T(8,128)(2,1)S(1)}, bf16[4,7,256,128]{3,2,1,0:T(8,128)(2,1)}, u32[]{:S(2)}) copy-start(bf16[4,7,256,128]{3,2,1,0:T(8,128)(2,1)} %get-tuple-element.154) | copy-start | bytes 5505028 | tf_op jit(solution)/shard_map/while
  375.7 7.0 %copy-start = (bf16[4,7,256,128]{3,2,1,0:T(8,128)(2,1)S(1)}, bf16[4,7,256,128]{3,2,1,0:T(8,128)(2,1)}, u32[]{:S(2)}) copy-start(bf16[4,7,256,128]{3,2,1,0:T(8,128)(2,1)} %get-tuple-element.154) | copy-start | bytes 5505028 | tf_op jit(solution)/shard_map/while
  397.8 7.0 %copy-start = (bf16[4,7,256,128]{3,2,1,0:T(8,128)(2,1)S(1)}, bf16[4,7,256,128]{3,2,1,0:T(8,128)(2,1)}, u32[]{:S(2)}) copy-start(bf16[4,7,256,128]{3,2,1,0:T(8,128)(2,1)} %get-tuple-element.154) | copy-start | bytes 5505028 | tf_op jit(solution)/shard_map/while
  419.8 7.0 %copy-start = (bf16[4,7,256,128]{3,2,1,0:T(8,128)(2,1)S(1)}, bf16[4,7,256,128]{3,2,1,0:T(8,128)(2,1)}, u32[]{:S(2)}) copy-start(bf16[4,7,256,128]{3,2,1,0:T(8,128)(2,1)} %get-tuple-element.154) | copy-start | bytes 5505028 | tf_op jit(solution)/shard_map/while
  441.9 7.0 %copy-start = (bf16[4,7,256,128]{3,2,1,0:T(8,128)(2,1)S(1)}, bf16[4,7,256,128]{3,2,1,0:T(8,128)(2,1)}, u32[]{:S(2)}) copy-start(bf16[4,7,256,128]{3,2,1,0:T(8,128)(2,1)} %get-tuple-element.154) | copy-start | bytes 5505028 | tf_op jit(solution)/shard_map/while
  464.0 7.0 %copy-start = (bf16[4,7,256,128]{3,2,1,0:T(8,128)(2,1)S(1)}, bf16[4,7,256,128]{3,2,1,0:T(8,128)(2,1)}, u32[]{:S(2)}) copy-start(bf16[4,7,256,128]{3,2,1,0:T(8,128)(2,1)} %get-tuple-element.154) | copy-start | bytes 5505028 | tf_op jit(solution)/shard_map/while
Sparse Core Ops, SparseCore 0:
  19.5 132.0 all-gather.2
  169.9 121.4 all-gather.4
where the time goes:
time: 588 us; the launch traced here: 586 us
  waiting for transfers between devices  259 us (44%)
  local copies, waits for them, and re-layouts  101 us (17%)
  matrix products  80.7 us (14%)
  blocking collectives  65.2 us (11%)
  other arithmetic  40.8 us (7%)
  starting transfers between devices  25.9 us (4%)
  between operations  13.6 us (2%)
    all_to_all x1, waiting for transfers between devices, body(): lax.all_to_all(split_shape(queries, seq_count), 'seq', split_axis=1, conc...  136 us
    all_to_all x1, waiting for transfers between devices, body(): lax.all_to_all(split_shape(values, seq_count), 'seq', split_axis=1, conca...  67.5 us
    all_to_all x1, waiting for transfers between devices, body(): lax.all_to_all(split_shape(keys, seq_count), 'seq', split_axis=1, concat_...  54 us
    all_to_all x1, blocking collectives, body(): lax.all_to_all(frame_order(attended_output.reshape(tok_dev, head_dev * DH...  42.6 us
    sub x6, matrix products, band_attend(): weights = jnp.exp(attention_scores - row_max)  41.8 us
    dot_general x6, matrix products, band_attend(): jnp.einsum('oyx,oxi->oyi', attention_probabilities, nearby_values, prefer...  25.6 us
    all_to_all x1, blocking collectives, body(): lax.all_to_all(final_rows, 'head', split_axis=0, concat_axis=1, tiled=True)  22.6 us
    select_n x12, other arithmetic, band_attend(): jnp.take(k_blocks, key_index, axis=0)  22.5 us
  transfers between devices with their start and end apart: 7, of which 3 were waited for; matrix products, arithmetic and copies ran while one was open for 34% of the time, Pallas kernels for 0%

commit v1 on v0

v1 whole, which is shorter than its diff:
```python
import functools
import math

import jax
import jax.numpy as jnp
from jax import lax
from jax.experimental import pallas as pl
from jax.experimental.pallas import tpu as pltpu
from jax.sharding import PartitionSpec as P

DH = 128
FRAMES = 16
BLK = 256
CHUNK = 16
LIMIT = 48 * 1024 * 1024


class Plan:
    def __init__(self, seq_count, tok, head_dev, koff):
        self.n = seq_count
        self.pairs = seq_count // 2
        self.tok = tok
        self.hd = head_dev
        self.cap = head_dev - 1
        self.s = (head_dev + 1) // 2
        self.koff = koff
        positions = tok * seq_count // FRAMES
        self.span_rows = min(tok, positions)
        self.spans = tok // self.span_rows
        self.quota = self.span_rows // seq_count
        self.halves = positions // self.span_rows
        self.piece = self.spans * 2 * self.quota
        self.groups = 2 * self.quota // CHUNK
        self.unit = self.pairs * self.spans * CHUNK
        self.blocks = tok // BLK
        self.total = self.blocks * seq_count
        self.at_pair = 0
        self.at_side = 1
        self.at_order = 2
        self.at_kind = self.at_order + 2 * self.s
        self.at_band = self.at_kind + 2 * self.s


def table_of(plan, head_kind, band_offsets):
    rank = lax.axis_index("seq")
    kinds = lax.dynamic_slice_in_dim(head_kind, lax.axis_index("head") * plan.hd, plan.hd)
    places = jnp.arange(plan.hd, dtype=jnp.int32)
    spatial = jnp.min(jnp.where(kinds == 0, places, plan.hd - 1))
    low = jnp.arange(plan.cap, dtype=jnp.int32)
    order = low + (low >= spatial).astype(jnp.int32)
    kind = jnp.where(low < spatial, kinds[:-1], kinds[1:])
    rest = 2 * plan.s - plan.cap
    return jnp.concatenate(
        [
            (rank // 2).reshape(1).astype(jnp.int32),
            (rank % 2).reshape(1).astype(jnp.int32),
            order,
            jnp.broadcast_to(spatial, (rest,)),
            kind.astype(jnp.int32),
            jnp.zeros((rest,), jnp.int32),
            band_offsets.reshape(-1),
        ]
    )


def pair_permute(plan, cells, k):
    return lax.ppermute(
        cells,
        "seq",
        [(2 * p + y, 2 * (p ^ k) + y) for p in range(plan.pairs) for y in range(2)],
    )


def side_permute(plan, cells):
    return lax.ppermute(cells, "seq", [(i, i ^ 1) for i in range(plan.n)])


def call(body, plan, grid, in_specs, out_specs, out_shape, name, scratch=(), cost=None):
    return pl.pallas_call(
        body,
        grid_spec=pltpu.PrefetchScalarGridSpec(
            num_scalar_prefetch=1,
            grid=grid,
            in_specs=in_specs,
            out_specs=out_specs,
            scratch_shapes=list(scratch),
        ),
        out_shape=out_shape,
        compiler_params=pltpu.CompilerParams(
            vmem_limit_bytes=LIMIT, dimension_semantics=("arbitrary",) * len(grid)
        ),
        cost_estimate=cost,
        name=name,
    )


def copy_cost(count):
    return pl.CostEstimate(flops=0, bytes_accessed=count, transcendentals=0)


def shape(*dims):
    return jax.ShapeDtypeStruct(dims, jnp.bfloat16)


def split_pieces(plan, table, cells, name):
    r2 = 2 * plan.quota

    def body(info, x_ref, *outs):
        pair = info[plan.at_pair]
        for k, out in enumerate(outs):
            for sp in range(plan.spans):
                start = pl.multiple_of(sp * plan.span_rows + (pair ^ k) * r2, r2)
                out[0, sp * r2 : (sp + 1) * r2, :] = x_ref[pl.ds(start, r2), :]

    return call(
        body,
        plan,
        (plan.cap,),
        [pl.BlockSpec((plan.tok, DH), lambda j, info: (0, info[plan.at_order + j]))],
        [pl.BlockSpec((1, plan.piece, DH), lambda j, info: (j, 0, 0))] * plan.pairs,
        [shape(plan.cap, plan.piece, DH)] * plan.pairs,
        name,
        cost=copy_cost(2 * 2 * plan.cap * plan.tok * DH),
    )(table, cells)


def share_slots(plan, table, pieces, cells, name):
    r2 = 2 * plan.quota
    s = plan.s

    def slot_of(t, info):
        side = info[plan.at_side]
        return jnp.where(t < s, (1 - side) * s + t, side * s + t - s)

    def body(info, *refs):
        pieces_in, x_ref = refs[: plan.pairs], refs[plan.pairs]
        send, keep = refs[plan.pairs + 1 :]
        t = pl.program_id(0)
        kind = info[plan.at_kind + slot_of(t, info)]

        def write(out):
            @pl.when(kind == 1)
            def _():
                for k in range(plan.pairs):
                    for sp in range(plan.spans):
                        for c in range(plan.groups):
                            row = c * plan.unit + (k * plan.spans + sp) * CHUNK
                            out[0, row : row + CHUNK, :] = pieces_in[k][
                                0, sp * r2 + c * CHUNK : sp * r2 + (c + 1) * CHUNK, :
                            ]

            @pl.when(kind != 1)
            def _():
                out[0] = x_ref[...]

        @pl.when(t < s)
        def _():
            write(send)

        @pl.when(t >= s)
        def _():
            write(keep)

    return call(
        body,
        plan,
        (2 * s,),
        [
            pl.BlockSpec(
                (1, plan.piece, DH),
                lambda t, info: (jnp.minimum(slot_of(t, info), plan.cap - 1), 0, 0),
            )
        ]
        * plan.pairs
        + [
            pl.BlockSpec(
                (plan.tok, DH), lambda t, info: (0, info[plan.at_order + slot_of(t, info)])
            )
        ],
        [
            pl.BlockSpec((1, plan.tok, DH), lambda t, info: (jnp.minimum(t, s - 1), 0, 0)),
            pl.BlockSpec((1, plan.tok, DH), lambda t, info: (jnp.maximum(t - s, 0), 0, 0)),
        ],
        [shape(s, plan.tok, DH)] * 2,
        name,
        cost=copy_cost(2 * 3 * 2 * s * plan.tok * DH),
    )(table, *pieces, cells)


def block_sources(plan, kind, side):
    sources = []
    for b in range(2 * plan.blocks):
        if kind == 1 and plan.halves == 1:
            first = b * plan.unit
            sources.append([(0, first, plan.unit), (1, first, plan.unit)])
        elif kind == 1:
            per = plan.quota // CHUNK
            d, rest = divmod(b, plan.halves * per)
            h, c = divmod(rest, per)
            sources.append([(0 if h == side else 1, (d * per + c) * BLK, BLK)])
        else:
            part, row = divmod(b, plan.blocks)
            sources.append([(0 if part == side else 1, row * BLK, BLK)])
    return sources


def each_case(plan, info, slot, use):
    kind = info[plan.at_kind + slot]
    side = info[plan.at_side]
    for a_kind in range(2):
        for a_side in range(2):

            @pl.when((kind == a_kind) & (side == a_side))
            def _():
                use(block_sources(plan, a_kind, a_side))


def join_blocks(plan, table, own, other, name):
    s = plan.s

    def body(info, own_ref, other_ref, low, high):
        slot = info[plan.at_side] * s + pl.program_id(0)

        def use(sources):
            for b, parts in enumerate(sources):
                out = low if b < plan.blocks else high
                row = (b % plan.blocks) * BLK
                for part, first, rows in parts:
                    src = own_ref if part == 0 else other_ref
                    out[0, row : row + rows, :] = src[0, first : first + rows, :]
                    row += rows

        each_case(plan, info, slot, use)

    spec = pl.BlockSpec((1, plan.tok, DH), lambda t, info: (t, 0, 0))
    return call(
        body,
        plan,
        (s,),
        [spec] * 2,
        [spec] * 2,
        [shape(s, plan.tok, DH)] * 2,
        name,
        cost=copy_cost(2 * 4 * s * plan.tok * DH),
    )(table, own, other)


def attend(plan, table, q_parts, k_parts, v_parts):
    s, koff, tok = plan.s, plan.koff, plan.tok
    factor = math.log2(math.e) / math.sqrt(DH)

    def body(info, q_own, q_oth, k0, k1, k2, k3, v0, v1, v2, v3, o_own, o_oth, qs, ks, vs, os):
        t = pl.program_id(0)
        side = info[plan.at_side]
        slot = side * s + t
        kind = info[plan.at_kind + slot]
        first_block = info[plan.at_pair] * (2 * plan.blocks)

        @pl.when(t == 0)
        def _():
            vs[:, DH:] = jnp.ones((4 * tok, DH), jnp.bfloat16)

        for i, (k_ref, v_ref) in enumerate(((k0, v0), (k1, v1), (k2, v2), (k3, v3))):
            ks[i * tok : (i + 1) * tok, :] = k_ref[0]
            vs[i * tok : (i + 1) * tok, :DH] = v_ref[0]

        def load(sources):
            for b, parts in enumerate(sources):
                row = b * BLK
                for part, first, rows in parts:
                    src = q_own if part == 0 else q_oth
                    qs[row : row + rows, :] = src[0, first : first + rows, :]
                    row += rows

        each_case(plan, info, slot, load)

        def block(b):
            q = qs[pl.ds(pl.multiple_of(b * BLK, BLK), BLK), :]
            rows, drops = [], []
            for j in range(koff):
                goal = b + info[plan.at_band + kind * koff + j]
                ok = (first_block + goal >= 0) & (first_block + goal < plan.total)
                rows.append(pl.multiple_of((jnp.where(ok, goal, b) + plan.blocks) * BLK, BLK))
                drops.append(jnp.where(ok, 0.0, 1e30).astype(jnp.float32))
            keys = jnp.concatenate([ks[pl.ds(r, BLK), :] for r in rows], axis=0)
            scores = lax.dot_general(
                q, keys, (((1,), (1,)), ((), ())), preferred_element_type=jnp.float32
            )
            top = jnp.max(scores, axis=1, keepdims=True) * factor
            probs = jnp.concatenate(
                [
                    jnp.exp2(scores[:, j * BLK : (j + 1) * BLK] * factor - (top + drops[j])).astype(
                        jnp.bfloat16
                    )
                    for j in range(koff)
                ],
                axis=1,
            )
            vals = jnp.concatenate([vs[pl.ds(r, BLK), :] for r in rows], axis=0)
            mix = jnp.dot(probs, vals, preferred_element_type=jnp.float32)
            os[pl.ds(pl.multiple_of(b * BLK, BLK), BLK), :] = (mix[:, :DH] / mix[:, DH:]).astype(
                jnp.bfloat16
            )

        @pl.loop(0, plan.blocks)
        def _(i):
            block(2 * i)
            block(2 * i + 1)

        def store(sources):
            for b, parts in enumerate(sources):
                row = b * BLK
                for part, first, rows in parts:
                    dst = o_own if part == 0 else o_oth
                    dst[0, first : first + rows, :] = os[row : row + rows, :]
                    row += rows

        each_case(plan, info, slot, store)

    spec = pl.BlockSpec((1, tok, DH), lambda t, info: (t, 0, 0))
    pairs_count = s * 2 * plan.blocks * BLK * koff * BLK
    return call(
        body,
        plan,
        (s,),
        [spec] * 10,
        [spec] * 2,
        [shape(s, tok, DH)] * 2,
        "attend",
        scratch=[
            pltpu.VMEM((2 * tok, DH), jnp.bfloat16),
            pltpu.VMEM((4 * tok, DH), jnp.bfloat16),
            pltpu.VMEM((4 * tok, 2 * DH), jnp.bfloat16),
            pltpu.VMEM((2 * tok, DH), jnp.bfloat16),
        ],
        cost=pl.CostEstimate(
            flops=4 * pairs_count * DH,
            bytes_accessed=12 * 2 * s * tok * DH,
            transcendentals=pairs_count,
        ),
    )(table, *q_parts, *k_parts, *v_parts)


def return_pieces(plan, table, own, other):
    r2 = 2 * plan.quota
    s = plan.s

    def body(info, own_ref, oth_ref, *outs):
        j = pl.program_id(0)
        mine = j // s == info[plan.at_side]

        def write(src):
            for k, out in enumerate(outs):
                for sp in range(plan.spans):
                    for c in range(plan.groups):
                        row = c * plan.unit + (k * plan.spans + sp) * CHUNK
                        out[0, sp * r2 + c * CHUNK : sp * r2 + (c + 1) * CHUNK, :] = src[
                            0, row : row + CHUNK, :
                        ]

        @pl.when(mine)
        def _():
            write(own_ref)

        @pl.when(jnp.logical_not(mine))
        def _():
            write(oth_ref)

    spec = pl.BlockSpec((1, plan.tok, DH), lambda j, info: (j % s, 0, 0))
    return call(
        body,
        plan,
        (plan.cap,),
        [spec] * 2,
        [pl.BlockSpec((1, plan.piece, DH), lambda j, info: (j, 0, 0))] * plan.pairs,
        [shape(plan.cap, plan.piece, DH)] * plan.pairs,
        "return_pieces",
        cost=copy_cost(2 * 3 * plan.cap * plan.tok * DH),
    )(table, own, other)


def final_rows(plan, table, pieces, own, other):
    r2 = 2 * plan.quota
    s = plan.s

    def body(info, own_ref, oth_ref, *refs):
        pieces_in, out = refs[: plan.pairs], refs[plan.pairs]
        j = pl.program_id(0)
        pair = info[plan.at_pair]
        kind = info[plan.at_kind + j]
        mine = j // s == info[plan.at_side]

        @pl.when(kind == 1)
        def _():
            for k in range(plan.pairs):
                for sp in range(plan.spans):
                    start = pl.multiple_of(sp * plan.span_rows + (pair ^ k) * r2, r2)
                    out[pl.ds(start, r2), :] = pieces_in[k][0, sp * r2 : (sp + 1) * r2, :]

        @pl.when((kind != 1) & mine)
        def _():
            out[...] = own_ref[0]

        @pl.when((kind != 1) & jnp.logical_not(mine))
        def _():
            out[...] = oth_ref[0]

    spec = pl.BlockSpec((1, plan.tok, DH), lambda j, info: (j % s, 0, 0))
    piece = pl.BlockSpec(
        (1, plan.piece, DH), lambda j, info: (jnp.minimum(j, plan.cap - 1), 0, 0)
    )
    return call(
        body,
        plan,
        (plan.hd,),
        [spec] * 2 + [piece] * plan.pairs,
        pl.BlockSpec((plan.tok, DH), lambda j, info: (0, info[plan.at_order + j])),
        shape(plan.tok, plan.hd * DH),
        "final_rows",
        cost=copy_cost(2 * 4 * plan.hd * plan.tok * DH),
    )(table, own, other, *pieces)


def project(rows, weights):
    groups, r, c = rows.shape
    seq, _, _, d = weights.shape
    step = math.lcm(d, 256) // d

    def body(x_ref, w_ref, out):
        total = jnp.zeros((r, step * d), jnp.float32)
        for g in range(groups):
            w = jnp.concatenate([w_ref[i, g] for i in range(step)], axis=1)
            total += jnp.dot(x_ref[g], w, preferred_element_type=jnp.float32)
        out[...] = total.astype(jnp.bfloat16)

    return pl.pallas_call(
        body,
        grid=(seq // step,),
        in_specs=[
            pl.BlockSpec((groups, r, c), lambda i: (0, 0, 0)),
            pl.BlockSpec((step, groups, c, d), lambda i: (i, 0, 0, 0)),
        ],
        out_specs=pl.BlockSpec((r, step * d), lambda i: (0, i)),
        out_shape=shape(r, seq * d),
        compiler_params=pltpu.CompilerParams(vmem_limit_bytes=LIMIT),
        cost_estimate=pl.CostEstimate(
            flops=2 * groups * r * c * seq * d,
            bytes_accessed=2 * (groups * r * c + seq * groups * c * d + r * seq * d),
            transcendentals=0,
        ),
        name="project",
    )(rows, weights)


def body(queries, keys, values, w_out, head_kind, band_offsets):
    tok = queries.shape[0]
    plan = Plan(lax.axis_size("seq"), tok, queries.shape[1] // DH, band_offsets.shape[1])
    group_count = lax.axis_size("head")
    table = table_of(plan, head_kind, band_offsets)

    weights = lax.all_gather(w_out, ("seq", "head"), axis=0, tiled=False)
    weights = weights.reshape(plan.n, group_count, *w_out.shape)

    def exchange(cells, name):
        pieces = split_pieces(plan, table, cells, "split_" + name)
        moved = [pieces[0]] + [pair_permute(plan, pieces[k], k) for k in range(1, plan.pairs)]
        send, keep = share_slots(plan, table, moved, cells, "share_" + name)
        return keep, side_permute(plan, send)

    up = [(i, i + 2) for i in range(plan.n - 2)]
    down = [(i + 2, i) for i in range(plan.n - 2)]

    def extend(parts, name):
        low, high = join_blocks(plan, table, *parts, "join_" + name)
        return lax.ppermute(high, "seq", up), low, high, lax.ppermute(low, "seq", down)

    k_parts = extend(exchange(keys, "k"), "k")
    v_parts = extend(exchange(values, "v"), "v")
    q_parts = exchange(queries, "q")
    o_own, o_oth = attend(plan, table, q_parts, k_parts, v_parts)
    o_back = side_permute(plan, o_oth)
    pieces = return_pieces(plan, table, o_own, o_back)
    moved = [pieces[0]] + [pair_permute(plan, pieces[k], k) for k in range(1, plan.pairs)]
    rows = final_rows(plan, table, moved, o_own, o_back)
    token_rows = lax.all_to_all(
        rows.reshape(group_count, tok // group_count, plan.hd * DH),
        "head",
        split_axis=0,
        concat_axis=0,
        tiled=True,
    )
    return project(token_rows, weights)


def solution(mesh):
    return jax.shard_map(
        body,
        mesh=mesh,
        in_specs=(P("seq", "head"), P("seq", "head"), P("seq", "head"), P("head", "seq"), P(), P()),
        out_specs=P(("seq", "head"), None),
        check_vma=False,
    )
```

time: 588 us -> 346 us (0.59)
  local copies, waits for them, and re-layouts: 101 us -> 5.24 us
  waiting for transfers between devices: 259 us -> 174 us
  matrix products: 80.7 us -> 0 us
  starting transfers between devices: 25.9 us -> 80.4 us
  Pallas kernels: 0 us -> 45.9 us
  blocking collectives: 65.2 us -> 22.7 us
  other arithmetic: 40.8 us -> 2.2 us
    all_to_all x3 -> x0, waiting for transfers between devices: 257 us -> none  [the longest x1 136 us: body(): lax.all_to_all(split_shape(queries, seq_count), 'seq', split_axis=1, conc...]
    ppermute x2 -> x20, waiting for transfers between devices: 0.01 us -> 173 us  [the longest x12 122 us: pair_permute(): lax.ppermute(cells, 'seq', [(2 * p + y, 2 * (p ^ k) + y) for p in range(p...]
    ppermute x2 -> x20, starting transfers between devices: 8.86 us -> 80.4 us  [the longest x12 43.4 us: pair_permute(): lax.ppermute(cells, 'seq', [(2 * p + y, 2 * (p ^ k) + y) for p in range(p...]
    pallas_call x0 -> x12, Pallas kernels: none -> 45.9 us  [the longest x1 25.6 us: attend(): call(body, plan, (s,), [spec] * 10, [spec] * 2, [shape(s, tok, DH)] * 2,...]
    all_to_all x2 -> x1, blocking collectives: 65.2 us -> 22.7 us  [body(): lax.all_to_all(rows.reshape(group_count, tok // group_count, plan.hd * DH...]
    sub x6 -> x0, matrix products: 41.8 us -> none  [band_attend(): weights = jnp.exp(attention_scores - row_max)]
    dot_general x7 -> x0, matrix products: 38.9 us -> none  [the longest x6 25.6 us: band_attend(): jnp.einsum('oyx,oxi->oyi', attention_probabilities, nearby_values, prefer...]
    select_n x15 -> x1, other arithmetic: 26.8 us -> 0.76 us  [table_of(): kind = jnp.where(low < spatial, kinds[:-1], kinds[1:])]
  transfers between devices with their start and end apart: 7 -> 21, of which waited for: 3 -> 13; matrix products, arithmetic and copies ran while one was open for 34% -> 1% of each run, Pallas kernels for 0% -> 10%
where the time goes in v1:
time: 346 us; the launch traced here: 344 us
  waiting for transfers between devices  174 us (50%)
  starting transfers between devices  80.4 us (23%)
  Pallas kernels  45.9 us (13%)
  blocking collectives  22.7 us (7%)
  between operations  13.6 us (4%)
  local copies, waits for them, and re-layouts  5.24 us (2%)
    ppermute x12, waiting for transfers between devices, pair_permute(): lax.ppermute(cells, 'seq', [(2 * p + y, 2 * (p ^ k) + y) for p in range(p...  122 us
    ppermute x12, starting transfers between devices, pair_permute(): lax.ppermute(cells, 'seq', [(2 * p + y, 2 * (p ^ k) + y) for p in range(p...  43.4 us
    ppermute x2, starting transfers between devices, extend(): lax.ppermute(high, 'seq', up)  31 us
    pallas_call x1, Pallas kernels, attend(): call(body, plan, (s,), [spec] * 10, [spec] * 2, [shape(s, tok, DH)] * 2,...  25.6 us
    all_to_all x1, blocking collectives, body(): lax.all_to_all(rows.reshape(group_count, tok // group_count, plan.hd * DH...  22.7 us
    ppermute x2, waiting for transfers between devices, extend(): lax.ppermute(high, 'seq', up)  22.3 us
    ppermute x4, waiting for transfers between devices, side_permute(): return lax.ppermute(cells, 'seq', [(i, i ^ 1) for i in range(plan.n)])  17.8 us
    ppermute x2, waiting for transfers between devices, extend(): lax.ppermute(low, 'seq', down)  10.7 us
  transfers between devices with their start and end apart: 21, of which 13 were waited for; matrix products, arithmetic and copies ran while one was open for 1% of the time, Pallas kernels for 10%

profile of v1, /device:TPU:0, one launch (start us, length us, event | category | flops | bytes accessed | tf_op | source)
XLA Modules:
  0.0 344.1 jit_solution(1766158479344517955)
XLA Ops:
  13.4 3.1 collective-permute-start.10
  16.5 2.6 collective-permute-start.11
  22.5 3.5 %collective-permute-start.5 = (bf16[5,256,128]{2,1,0:T(8,128)(2,1)S(1)}, bf16[5,256,128]{2,1,0:T(8,128)(2,1)S(1)}, u32[]{:S(2)}, u32[]{:S(2)}) collective-permute-start(bf16[5,256,128]{2,1,0:T(8,128)(2,1)S(1)} %get-tuple-element.41), channel_id=1, source_target_pairs={{0,16},{4,20},{8,24},{12,28},{16,0},{20,4},{24,8},{28,12},{1,17},{... | collective-permute-start | bytes 983048 | tf_op jit(solution)/shard_map/ppermute | solution.py:67
  26.0 11.6 %collective-permute-done.10.refs_1_ = bf16[5,256,128]{2,1,0:T(8,128)(2,1)S(1)} collective-permute-done((bf16[5,256,128]{2,1,0:T(8,128)(2,1)S(1)}, bf16[5,256,128]{2,1,0:T(8,128)(2,1)S(1)}, u32[]{:S(2)}, u32[]{:S(2)}) %collective-permute-start.10) | collective-permute-done | bytes 327712 | tf_op jit(solution)/shard_map/ppermute | solution.py:67
  37.6 14.8 %collective-permute-start.6 = (bf16[5,256,128]{2,1,0:T(8,128)(2,1)S(1)}, bf16[5,256,128]{2,1,0:T(8,128)(2,1)S(1)}, u32[]{:S(2)}, u32[]{:S(2)}) collective-permute-start(bf16[5,256,128]{2,1,0:T(8,128)(2,1)S(1)} %get-tuple-element.42), channel_id=1, source_target_pairs={{0,24},{4,28},{8,16},{12,20},{16,8},{20,12},{24,0},{28,4},{1,25},{... | collective-permute-start | bytes 983048 | tf_op jit(solution)/shard_map/ppermute | solution.py:67
  55.5 2.9 collective-permute-done.4.refs_1_
  58.3 44.7 %collective-permute-done.5.refs_2_ = bf16[5,256,128]{2,1,0:T(8,128)(2,1)S(1)} collective-permute-done((bf16[5,256,128]{2,1,0:T(8,128)(2,1)S(1)}, bf16[5,256,128]{2,1,0:T(8,128)(2,1)S(1)}, u32[]{:S(2)}, u32[]{:S(2)}) %collective-permute-start.5) | collective-permute-done | bytes 327712 | tf_op jit(solution)/shard_map/ppermute | solution.py:67
  106.9 11.5 %collective-permute-start = (bf16[5,256,128]{2,1,0:T(8,128)(2,1)S(1)}, bf16[5,256,128]{2,1,0:T(8,128)(2,1)S(1)}, u32[]{:S(2)}, u32[]{:S(2)}) collective-permute-start(bf16[5,256,128]{2,1,0:T(8,128)(2,1)S(1)} %get-tuple-element.34), channel_id=1, source_target_pairs={{0,8},{4,12},{8,0},{12,4},{16,24},{20,28},{24,16},{28,20},{1,9},{5... | collective-permute-start | bytes 983048 | tf_op jit(solution)/shard_map/ppermute | solution.py:67
  120.9 22.5 %collective-permute-done.refs_1_ = bf16[5,256,128]{2,1,0:T(8,128)(2,1)S(1)} collective-permute-done((bf16[5,256,128]{2,1,0:T(8,128)(2,1)S(1)}, bf16[5,256,128]{2,1,0:T(8,128)(2,1)S(1)}, u32[]{:S(2)}, u32[]{:S(2)}) %collective-permute-start) | collective-permute-done | bytes 327712 | tf_op jit(solution)/shard_map/ppermute | solution.py:67
  143.3 16.2 %collective-permute-done.1.refs_2_ = bf16[5,256,128]{2,1,0:T(8,128)(2,1)S(1)} collective-permute-done((bf16[5,256,128]{2,1,0:T(8,128)(2,1)S(1)}, bf16[5,256,128]{2,1,0:T(8,128)(2,1)S(1)}, u32[]{:S(2)}, u32[]{:S(2)}) %collective-permute-start.1) | collective-permute-done | bytes 327712 | tf_op jit(solution)/shard_map/ppermute | solution.py:67
  159.5 2.9 collective-permute-done.2.refs_3_
  164.6 26.4 %collective-permute-start.14 = (bf16[3,1024,128]{2,1,0:T(8,128)(2,1)S(1)}, bf16[3,1024,128]{2,1,0:T(8,128)(2,1)S(1)}, u32[]{:S(2)}, u32[]{:S(2)}) collective-permute-start(bf16[3,1024,128]{2,1,0:T(8,128)(2,1)S(1)} %get-tuple-element.53.v2), channel_id=1, source_target_pairs={{0,8},{4,12},{8,16},{12,20},{16,24},{20,28},{1,9},{5,13},{9,17},{1... | collective-permute-start | bytes 2359304 | tf_op jit(solution)/shard_map/ppermute | solution.py:475
  193.1 4.6 %collective-permute-start.8 = (bf16[3,1024,128]{2,1,0:T(8,128)(2,1)S(1)}, bf16[3,1024,128]{2,1,0:T(8,128)(2,1)S(1)}, u32[]{:S(2)}, u32[]{:S(2)}) collective-permute-start(bf16[3,1024,128]{2,1,0:T(8,128)(2,1)S(1)} %get-tuple-element.45.k2), channel_id=1, source_target_pairs={{0,8},{4,12},{8,16},{12,20},{16,24},{20,28},{1,9},{5,13},{9,17},{1... | collective-permute-start | bytes 2359304 | tf_op jit(solution)/shard_map/ppermute | solution.py:475
  199.0 12.7 %collective-permute-done.14.v0 = bf16[3,1024,128]{2,1,0:T(8,128)(2,1)S(1)} collective-permute-done((bf16[3,1024,128]{2,1,0:T(8,128)(2,1)S(1)}, bf16[3,1024,128]{2,1,0:T(8,128)(2,1)S(1)}, u32[]{:S(2)}, u32[]{:S(2)}) %collective-permute-start.14) | collective-permute-done | bytes 786464 | tf_op jit(solution)/shard_map/ppermute | solution.py:475
  211.7 5.3 %collective-permute-done.15.v3 = bf16[3,1024,128]{2,1,0:T(8,128)(2,1)S(1)} collective-permute-done((bf16[3,1024,128]{2,1,0:T(8,128)(2,1)S(1)}, bf16[3,1024,128]{2,1,0:T(8,128)(2,1)S(1)}, u32[]{:S(2)}, u32[]{:S(2)}) %collective-permute-start.15) | collective-permute-done | bytes 786464 | tf_op jit(solution)/shard_map/ppermute | solution.py:475
  217.0 9.6 %collective-permute-done.8.k0 = bf16[3,1024,128]{2,1,0:T(8,128)(2,1)S(1)} collective-permute-done((bf16[3,1024,128]{2,1,0:T(8,128)(2,1)S(1)}, bf16[3,1024,128]{2,1,0:T(8,128)(2,1)S(1)}, u32[]{:S(2)}, u32[]{:S(2)}) %collective-permute-start.8) | collective-permute-done | bytes 786464 | tf_op jit(solution)/shard_map/ppermute | solution.py:475
  226.6 5.4 %collective-permute-done.9.k3 = bf16[3,1024,128]{2,1,0:T(8,128)(2,1)S(1)} collective-permute-done((bf16[3,1024,128]{2,1,0:T(8,128)(2,1)S(1)}, bf16[3,1024,128]{2,1,0:T(8,128)(2,1)S(1)}, u32[]{:S(2)}, u32[]{:S(2)}) %collective-permute-start.9) | collective-permute-done | bytes 786464 | tf_op jit(solution)/shard_map/ppermute | solution.py:475
  232.9 25.6 %attend.1 = (bf16[3,1024,128]{2,1,0:T(8,128)(2,1)S(1)}, bf16[3,1024,128]{2,1,0:T(8,128)(2,1)S(1)}) custom-call(s32[28]{0:T(128)S(1)} %concatenate.3.info, bf16[3,1024,128]{2,1,0:T(8,128)(2,1)S(1)} %get-tuple-element.37.q_own, bf16[3,1024,128]{2,1,0:T(8,128)(2,1)S(1)} %collective-permute-done.3.q_oth, bf16[3,1024,128]{2,1,0:T(8,128)(2,1)S(1)} %collective-permute-done.8.k0, ...), custom_call_target="tpu_custom_call" | custom-call | flops 5637144576 | bytes 9437184 | tf_op jit(solution)/shard_map/attend/pallas_call | solution.py:322
  258.6 17.8 %collective-permute-done.16.oth_ref = bf16[3,1024,128]{2,1,0:T(8,128)(2,1)S(1)} collective-permute-done((bf16[3,1024,128]{2,1,0:T(8,128)(2,1)S(1)}, bf16[3,1024,128]{2,1,0:T(8,128)(2,1)S(1)}, u32[]{:S(2)}, u32[]{:S(2)}) %collective-permute-start.16) | collective-permute-done | bytes 786464 | tf_op jit(solution)/shard_map/ppermute | solution.py:75
  278.9 2.7 collective-permute-start.19
  281.6 7.8 %collective-permute-done.17.refs_1_ = bf16[5,256,128]{2,1,0:T(8,128)(2,1)S(1)} collective-permute-done((bf16[5,256,128]{2,1,0:T(8,128)(2,1)S(1)}, bf16[5,256,128]{2,1,0:T(8,128)(2,1)S(1)}, u32[]{:S(2)}, u32[]{:S(2)}) %collective-permute-start.17) | collective-permute-done | bytes 327712 | tf_op jit(solution)/shard_map/ppermute | solution.py:67
  289.4 13.9 %collective-permute-done.18.refs_2_ = bf16[5,256,128]{2,1,0:T(8,128)(2,1)S(1)} collective-permute-done((bf16[5,256,128]{2,1,0:T(8,128)(2,1)S(1)}, bf16[5,256,128]{2,1,0:T(8,128)(2,1)S(1)}, u32[]{:S(2)}, u32[]{:S(2)}) %collective-permute-start.18) | collective-permute-done | bytes 327712 | tf_op jit(solution)/shard_map/ppermute | solution.py:67
  304.5 22.7 %all_to_all.5.x_ref = bf16[4,256,768]{2,1,0:T(8,128)(2,1)S(1)} all-to-all(bf16[4,256,768]{2,1,0:T(8,128)(2,1)S(1)} %bitcast.5), channel_id=1, replica_groups=mesh['seq'=8,'head'=4] {'head'}, dimensions={0} | all-to-all | bytes 3145728 | tf_op jit(solution)/shard_map/all_to_all | solution.py:485
  327.2 10.1 %project.1 = bf16[256,3072]{1,0:T(8,128)(2,1)} custom-call(bf16[4,256,768]{2,1,0:T(8,128)(2,1)S(1)} %all_to_all.5.x_ref, bf16[8,4,768,384]{3,2,1,0:T(8,128)(2,1)} %bitcast.6), custom_call_target="tpu_custom_call" | custom-call | flops 4831838208 | bytes 22020096 | tf_op jit(solution)/shard_map/project/pallas_call | solution.py:436
  (54 shorter events, 29.7 us)
Async XLA Ops:
  6.5 320.6 %all-gather.3.cloned.1.call-start = ((), (), s32[]{:S(2)}) async-start(), calls=%async_computation.1 | async-start | bytes 19464192 | tf_op jit(solution)/shard_map/all_gather | solution.py:461
  13.4 24.2 %collective-permute-start.10 = (bf16[5,256,128]{2,1,0:T(8,128)(2,1)S(1)}, bf16[5,256,128]{2,1,0:T(8,128)(2,1)S(1)}, u32[]{:S(2)}, u32[]{:S(2)}) collective-permute-start(bf16[5,256,128]{2,1,0:T(8,128)(2,1)S(1)} %get-tuple-element.48), channel_id=1, source_target_pairs={{0,8},{4,12},{8,0},{12,4},{16,24},{20,28},{24,16},{28,20},{1,9},{5... | collective-permute-start | bytes 983048 | tf_op jit(solution)/shard_map/ppermute | solution.py:67
  16.5 35.9 %collective-permute-start.11 = (bf16[5,256,128]{2,1,0:T(8,128)(2,1)S(1)}, bf16[5,256,128]{2,1,0:T(8,128)(2,1)S(1)}, u32[]{:S(2)}, u32[]{:S(2)}) collective-permute-start(bf16[5,256,128]{2,1,0:T(8,128)(2,1)S(1)} %get-tuple-element.49), channel_id=1, source_target_pairs={{0,16},{4,20},{8,24},{12,28},{16,0},{20,4},{24,8},{28,12},{1,17},{... | collective-permute-start | bytes 983048 | tf_op jit(solution)/shard_map/ppermute | solution.py:67
  19.1 33.4 %collective-permute-start.12 = (bf16[5,256,128]{2,1,0:T(8,128)(2,1)S(1)}, bf16[5,256,128]{2,1,0:T(8,128)(2,1)S(1)}, u32[]{:S(2)}, u32[]{:S(2)}) collective-permute-start(bf16[5,256,128]{2,1,0:T(8,128)(2,1)S(1)} %get-tuple-element.50), channel_id=1, source_target_pairs={{0,24},{4,28},{8,16},{12,20},{16,8},{20,12},{24,0},{28,4},{1,25},{... | collective-permute-start | bytes 983048 | tf_op jit(solution)/shard_map/ppermute | solution.py:67
  21.6 36.8 %collective-permute-start.4 = (bf16[5,256,128]{2,1,0:T(8,128)(2,1)S(1)}, bf16[5,256,128]{2,1,0:T(8,128)(2,1)S(1)}, u32[]{:S(2)}, u32[]{:S(2)}) collective-permute-start(bf16[5,256,128]{2,1,0:T(8,128)(2,1)S(1)} %get-tuple-element.40), channel_id=1, source_target_pairs={{0,8},{4,12},{8,0},{12,4},{16,24},{20,28},{24,16},{28,20},{1,9},{5... | collective-permute-start | bytes 983048 | tf_op jit(solution)/shard_map/ppermute | solution.py:67
  22.5 80.5 %collective-permute-start.5 = (bf16[5,256,128]{2,1,0:T(8,128)(2,1)S(1)}, bf16[5,256,128]{2,1,0:T(8,128)(2,1)S(1)}, u32[]{:S(2)}, u32[]{:S(2)}) collective-permute-start(bf16[5,256,128]{2,1,0:T(8,128)(2,1)S(1)} %get-tuple-element.41), channel_id=1, source_target_pairs={{0,16},{4,20},{8,24},{12,28},{16,0},{20,4},{24,8},{28,12},{1,17},{... | collective-permute-start | bytes 983048 | tf_op jit(solution)/shard_map/ppermute | solution.py:67
  37.6 65.4 %collective-permute-start.6 = (bf16[5,256,128]{2,1,0:T(8,128)(2,1)S(1)}, bf16[5,256,128]{2,1,0:T(8,128)(2,1)S(1)}, u32[]{:S(2)}, u32[]{:S(2)}) collective-permute-start(bf16[5,256,128]{2,1,0:T(8,128)(2,1)S(1)} %get-tuple-element.42), channel_id=1, source_target_pairs={{0,24},{4,28},{8,16},{12,20},{16,8},{20,12},{24,0},{28,4},{1,25},{... | collective-permute-start | bytes 983048 | tf_op jit(solution)/shard_map/ppermute | solution.py:67
  53.7 52.1 %copy-start.3 = (bf16[1024,768]{1,0:T(8,128)(2,1)S(1)}, bf16[1024,768]{1,0:T(8,128)(2,1)}, u32[]{:S(2)}) copy-start(bf16[1024,768]{1,0:T(8,128)(2,1)} %refs_4_.3) | copy-start | bytes 4718596
  53.8 110.1 %collective-permute-start.13 = (bf16[3,1024,128]{2,1,0:T(8,128)(2,1)S(1)}, bf16[3,1024,128]{2,1,0:T(8,128)(2,1)S(1)}, u32[]{:S(2)}, u32[]{:S(2)}) collective-permute-start(bf16[3,1024,128]{2,1,0:T(8,128)(2,1)S(1)} %get-tuple-element.52), channel_id=1, source_target_pairs={{0,4},{4,0},{8,12},{12,8},{16,20},{20,16},{24,28},{28,24},{1,5},{5... | collective-permute-start | bytes 2359304 | tf_op jit(solution)/shard_map/ppermute | solution.py:75
  104.3 88.0 %collective-permute-start.7 = (bf16[3,1024,128]{2,1,0:T(8,128)(2,1)S(1)}, bf16[3,1024,128]{2,1,0:T(8,128)(2,1)S(1)}, u32[]{:S(2)}, u32[]{:S(2)}) collective-permute-start(bf16[3,1024,128]{2,1,0:T(8,128)(2,1)S(1)} %get-tuple-element.44), channel_id=1, source_target_pairs={{0,4},{4,0},{8,12},{12,8},{16,20},{20,16},{24,28},{28,24},{1,5},{5... | collective-permute-start | bytes 2359304 | tf_op jit(solution)/shard_map/ppermute | solution.py:75
  106.9 36.4 %collective-permute-start = (bf16[5,256,128]{2,1,0:T(8,128)(2,1)S(1)}, bf16[5,256,128]{2,1,0:T(8,128)(2,1)S(1)}, u32[]{:S(2)}, u32[]{:S(2)}) collective-permute-start(bf16[5,256,128]{2,1,0:T(8,128)(2,1)S(1)} %get-tuple-element.34), channel_id=1, source_target_pairs={{0,8},{4,12},{8,0},{12,4},{16,24},{20,28},{24,16},{28,20},{1,9},{5... | collective-permute-start | bytes 983048 | tf_op jit(solution)/shard_map/ppermute | solution.py:67
  118.4 41.2 %collective-permute-start.1 = (bf16[5,256,128]{2,1,0:T(8,128)(2,1)S(1)}, bf16[5,256,128]{2,1,0:T(8,128)(2,1)S(1)}, u32[]{:S(2)}, u32[]{:S(2)}) collective-permute-start(bf16[5,256,128]{2,1,0:T(8,128)(2,1)S(1)} %get-tuple-element.35), channel_id=1, source_target_pairs={{0,16},{4,20},{8,24},{12,28},{16,0},{20,4},{24,8},{28,12},{1,17},{... | collective-permute-start | bytes 983048 | tf_op jit(solution)/shard_map/ppermute | solution.py:67
  119.5 43.0 %collective-permute-start.2 = (bf16[5,256,128]{2,1,0:T(8,128)(2,1)S(1)}, bf16[5,256,128]{2,1,0:T(8,128)(2,1)S(1)}, u32[]{:S(2)}, u32[]{:S(2)}) collective-permute-start(bf16[5,256,128]{2,1,0:T(8,128)(2,1)S(1)} %get-tuple-element.36), channel_id=1, source_target_pairs={{0,24},{4,28},{8,16},{12,20},{16,8},{20,12},{24,0},{28,4},{1,25},{... | collective-permute-start | bytes 983048 | tf_op jit(solution)/shard_map/ppermute | solution.py:67
  163.7 35.3 %collective-permute-start.3 = (bf16[3,1024,128]{2,1,0:T(8,128)(2,1)S(1)}, bf16[3,1024,128]{2,1,0:T(8,128)(2,1)S(1)}, u32[]{:S(2)}, u32[]{:S(2)}) collective-permute-start(bf16[3,1024,128]{2,1,0:T(8,128)(2,1)S(1)} %get-tuple-element.38), channel_id=1, source_target_pairs={{0,4},{4,0},{8,12},{12,8},{16,20},{20,16},{24,28},{28,24},{1,5},{5... | collective-permute-start | bytes 2359304 | tf_op jit(solution)/shard_map/ppermute | solution.py:75
  164.6 67.5 %copy-start.4 = (bf16[3,1024,128]{2,1,0:T(8,128)(2,1)}, bf16[3,1024,128]{2,1,0:T(8,128)(2,1)S(1)}, u32[]{:S(2)}) copy-start(bf16[3,1024,128]{2,1,0:T(8,128)(2,1)S(1)} %get-tuple-element.54.v1) | copy-start | bytes 2359300
  164.6 67.5 %copy-start.5 = (bf16[3,1024,128]{2,1,0:T(8,128)(2,1)}, bf16[3,1024,128]{2,1,0:T(8,128)(2,1)S(1)}, u32[]{:S(2)}) copy-start(bf16[3,1024,128]{2,1,0:T(8,128)(2,1)S(1)} %get-tuple-element.53.v2) | copy-start | bytes 2359300
  164.6 47.1 %collective-permute-start.14 = (bf16[3,1024,128]{2,1,0:T(8,128)(2,1)S(1)}, bf16[3,1024,128]{2,1,0:T(8,128)(2,1)S(1)}, u32[]{:S(2)}, u32[]{:S(2)}) collective-permute-start(bf16[3,1024,128]{2,1,0:T(8,128)(2,1)S(1)} %get-tuple-element.53.v2), channel_id=1, source_target_pairs={{0,8},{4,12},{8,16},{12,20},{16,24},{20,28},{1,9},{5,13},{9,17},{1... | collective-permute-start | bytes 2359304 | tf_op jit(solution)/shard_map/ppermute | solution.py:475
  191.0 26.0 %collective-permute-start.15 = (bf16[3,1024,128]{2,1,0:T(8,128)(2,1)S(1)}, bf16[3,1024,128]{2,1,0:T(8,128)(2,1)S(1)}, u32[]{:S(2)}, u32[]{:S(2)}) collective-permute-start(bf16[3,1024,128]{2,1,0:T(8,128)(2,1)S(1)} %get-tuple-element.54.v1), channel_id=1, source_target_pairs={{8,0},{12,4},{16,8},{20,12},{24,16},{28,20},{9,1},{13,5},{17,9},{2... | collective-permute-start | bytes 2359304 | tf_op jit(solution)/shard_map/ppermute | solution.py:475
  193.1 33.5 %collective-permute-start.8 = (bf16[3,1024,128]{2,1,0:T(8,128)(2,1)S(1)}, bf16[3,1024,128]{2,1,0:T(8,128)(2,1)S(1)}, u32[]{:S(2)}, u32[]{:S(2)}) collective-permute-start(bf16[3,1024,128]{2,1,0:T(8,128)(2,1)S(1)} %get-tuple-element.45.k2), channel_id=1, source_target_pairs={{0,8},{4,12},{8,16},{12,20},{16,24},{20,28},{1,9},{5,13},{9,17},{1... | collective-permute-start | bytes 2359304 | tf_op jit(solution)/shard_map/ppermute | solution.py:475
  197.7 34.3 %collective-permute-start.9 = (bf16[3,1024,128]{2,1,0:T(8,128)(2,1)S(1)}, bf16[3,1024,128]{2,1,0:T(8,128)(2,1)S(1)}, u32[]{:S(2)}, u32[]{:S(2)}) collective-permute-start(bf16[3,1024,128]{2,1,0:T(8,128)(2,1)S(1)} %get-tuple-element.46.k1), channel_id=1, source_target_pairs={{8,0},{12,4},{16,8},{20,12},{24,16},{28,20},{9,1},{13,5},{17,9},{2... | collective-permute-start | bytes 2359304 | tf_op jit(solution)/shard_map/ppermute | solution.py:475
  258.5 17.8 %collective-permute-start.16 = (bf16[3,1024,128]{2,1,0:T(8,128)(2,1)S(1)}, bf16[3,1024,128]{2,1,0:T(8,128)(2,1)S(1)}, u32[]{:S(2)}, u32[]{:S(2)}) collective-permute-start(bf16[3,1024,128]{2,1,0:T(8,128)(2,1)S(1)} %get-tuple-element.56), channel_id=1, source_target_pairs={{0,4},{4,0},{8,12},{12,8},{16,20},{20,16},{24,28},{28,24},{1,5},{5... | collective-permute-start | bytes 2359304 | tf_op jit(solution)/shard_map/ppermute | solution.py:75
  277.1 12.3 %collective-permute-start.17 = (bf16[5,256,128]{2,1,0:T(8,128)(2,1)S(1)}, bf16[5,256,128]{2,1,0:T(8,128)(2,1)S(1)}, u32[]{:S(2)}, u32[]{:S(2)}) collective-permute-start(bf16[5,256,128]{2,1,0:T(8,128)(2,1)S(1)} %get-tuple-element.58), channel_id=1, source_target_pairs={{0,8},{4,12},{8,0},{12,4},{16,24},{20,28},{24,16},{28,20},{1,9},{5... | collective-permute-start | bytes 983048 | tf_op jit(solution)/shard_map/ppermute | solution.py:67
  278.1 25.2 %collective-permute-start.18 = (bf16[5,256,128]{2,1,0:T(8,128)(2,1)S(1)}, bf16[5,256,128]{2,1,0:T(8,128)(2,1)S(1)}, u32[]{:S(2)}, u32[]{:S(2)}) collective-permute-start(bf16[5,256,128]{2,1,0:T(8,128)(2,1)S(1)} %get-tuple-element.59), channel_id=1, source_target_pairs={{0,16},{4,20},{8,24},{12,28},{16,0},{20,4},{24,8},{28,12},{1,17},{... | collective-permute-start | bytes 983048 | tf_op jit(solution)/shard_map/ppermute | solution.py:67
  278.9 24.4 %collective-permute-start.19 = (bf16[5,256,128]{2,1,0:T(8,128)(2,1)S(1)}, bf16[5,256,128]{2,1,0:T(8,128)(2,1)S(1)}, u32[]{:S(2)}, u32[]{:S(2)}) collective-permute-start(bf16[5,256,128]{2,1,0:T(8,128)(2,1)S(1)} %get-tuple-element.60), channel_id=1, source_target_pairs={{0,24},{4,28},{8,16},{12,20},{16,8},{20,12},{24,0},{28,4},{1,25},{... | collective-permute-start | bytes 983048 | tf_op jit(solution)/shard_map/ppermute | solution.py:67
  (6 other events, 79.2 us)
Sparse Core Ops, SparseCore 0:
  10.3 195.7 all-gather.2

commit v2 on v1

v2 whole, which is shorter than its diff:
```python
import functools
import math

import jax
import jax.numpy as jnp
from jax import lax
from jax.experimental import pallas as pl
from jax.experimental.pallas import tpu as pltpu
from jax.sharding import PartitionSpec as P

DH = 128
FRAMES = 16
BLK = 256
CHUNK = 16
LIMIT = 48 * 1024 * 1024


class Plan:
    def __init__(self, seq_count, group_count, tok, head_dev, koff):
        self.n = seq_count
        self.g = group_count
        self.pairs = seq_count // 2
        self.tok = tok
        self.hd = head_dev
        self.cap = head_dev - 1
        self.s = (head_dev + 1) // 2
        self.koff = koff
        positions = tok * seq_count // FRAMES
        self.span_rows = min(tok, positions)
        self.spans = tok // self.span_rows
        self.quota = self.span_rows // seq_count
        self.halves = positions // self.span_rows
        self.piece = self.spans * 2 * self.quota
        self.groups = 2 * self.quota // CHUNK
        self.unit = self.pairs * self.spans * CHUNK
        self.blocks = tok // BLK
        self.total = self.blocks * seq_count
        self.pair_groups = [[2 * p + y for p in range(self.pairs)] for y in range(2)]

    def exchanged(self, wave):
        return len([j for j in (wave, self.s + wave) if j < self.cap])


class Info:
    def __init__(self, plan, place, kinds, bands):
        self.plan, self.kinds, self.bands = plan, kinds, bands
        self.pair, self.side, self.group = place[0], place[1], place[2]

    def spatial(self, group):
        found = self.plan.hd - 1
        for j in reversed(range(self.plan.hd)):
            found = jnp.where(self.kinds[group * self.plan.hd + j] == 0, j, found)
        return found

    def head(self, slot, group=None):
        spatial = self.spatial(self.group if group is None else group)
        return jnp.where(
            slot < self.plan.cap, slot + jnp.where(slot >= spatial, 1, 0), spatial
        )

    def kind(self, slot):
        kind = self.kinds[self.group * self.plan.hd + self.head(slot)]
        return jnp.where(slot < self.plan.cap, kind, 0)


SCALARS = 3


def call(body, plan, scalars, grid, in_specs, out_specs, out_shape, name, scratch=(), cost=None):
    def with_info(*refs):
        body(Info(plan, *refs[:SCALARS]), *refs[SCALARS:])

    def wrap(spec):
        index_map = spec.index_map
        arity = len(grid)
        return pl.BlockSpec(
            spec.block_shape,
            lambda *args: index_map(*args[:arity], Info(plan, *args[arity:])),
        )

    in_specs = [wrap(x) for x in in_specs]
    out_specs = [wrap(x) for x in out_specs] if isinstance(out_specs, list) else wrap(out_specs)
    run = pl.pallas_call(
        with_info,
        grid_spec=pltpu.PrefetchScalarGridSpec(
            num_scalar_prefetch=SCALARS,
            grid=grid,
            in_specs=in_specs,
            out_specs=out_specs,
            scratch_shapes=list(scratch),
        ),
        out_shape=out_shape,
        compiler_params=pltpu.CompilerParams(
            vmem_limit_bytes=LIMIT, dimension_semantics=("arbitrary",) * len(grid)
        ),
        cost_estimate=cost,
        name=name,
    )
    return functools.partial(run, *scalars)


def copy_cost(count):
    return pl.CostEstimate(flops=0, bytes_accessed=count, transcendentals=0)


def shape(*dims):
    return jax.ShapeDtypeStruct(dims, jnp.bfloat16)


def whole(*dims):
    return pl.BlockSpec(dims, lambda *_: (0,) * len(dims))


def side_permute(plan, cells):
    return lax.ppermute(cells, "seq", [(i, i ^ 1) for i in range(plan.n)])


def pair_permute(plan, cells, k):
    return lax.ppermute(
        cells,
        "seq",
        [(2 * p + y, 2 * (p ^ k) + y) for p in range(plan.pairs) for y in range(2)],
    )


def pair_exchange(plan, pieces):
    return [pieces[0]] + [pair_permute(plan, pieces[k], k) for k in range(1, plan.pairs)]


def slot_spec(plan, slot_of):
    return pl.BlockSpec((plan.tok, DH), lambda t, info: (0, info.head(slot_of(t, info))))


def split_pieces(plan, scalars, cells, name):
    r2 = 2 * plan.quota

    def body(info, x_ref, *outs):
        for k, out in enumerate(outs):
            for sp in range(plan.spans):
                start = pl.multiple_of(sp * plan.span_rows + (info.pair ^ k) * r2, r2)
                out[0, sp * r2 : (sp + 1) * r2, :] = x_ref[pl.ds(start, r2), :]

    return call(
        body,
        plan,
        scalars,
        (plan.cap,),
        [slot_spec(plan, lambda t, info: t)],
        [pl.BlockSpec((1, plan.piece, DH), lambda j, info: (j, 0, 0))] * plan.pairs,
        [shape(plan.cap, plan.piece, DH)] * plan.pairs,
        "split_" + name,
        cost=copy_cost(4 * plan.cap * plan.tok * DH),
    )(cells)


def share_slots(plan, scalars, pieces, cells, name):
    r2 = 2 * plan.quota
    s = plan.s

    def slot_of(t, info):
        return jnp.where(t < s, (1 - info.side) * s + t, info.side * s + t - s)

    def body(info, *refs):
        pieces_in, x_ref = refs[: plan.pairs], refs[plan.pairs]
        send, keep = refs[plan.pairs + 1 :]
        t = pl.program_id(0)
        kind = info.kind(slot_of(t, info))

        def write(out):
            @pl.when(kind == 1)
            def _():
                for k in range(plan.pairs):
                    for sp in range(plan.spans):
                        for c in range(plan.groups):
                            row = c * plan.unit + (k * plan.spans + sp) * CHUNK
                            first = sp * r2 + c * CHUNK
                            out[0, row : row + CHUNK, :] = pieces_in[k][0, first : first + CHUNK, :]

            @pl.when(kind != 1)
            def _():
                out[0] = x_ref[...]

        @pl.when(t < s)
        def _():
            write(send)

        @pl.when(t >= s)
        def _():
            write(keep)

    piece = pl.BlockSpec(
        (1, plan.piece, DH), lambda t, info: (jnp.minimum(slot_of(t, info), plan.cap - 1), 0, 0)
    )
    return call(
        body,
        plan,
        scalars,
        (2 * s,),
        [piece] * plan.pairs + [slot_spec(plan, slot_of)],
        [
            pl.BlockSpec((1, plan.tok, DH), lambda t, info: (jnp.minimum(t, s - 1), 0, 0)),
            pl.BlockSpec((1, plan.tok, DH), lambda t, info: (jnp.maximum(t - s, 0), 0, 0)),
        ],
        [shape(s, plan.tok, DH)] * 2,
        "share_" + name,
        cost=copy_cost(12 * s * plan.tok * DH),
    )(*pieces, cells)


def block_sources(plan, kind, side):
    sources = []
    for b in range(2 * plan.blocks):
        if kind == 1 and plan.halves == 1:
            first = b * plan.unit
            sources.append([(0, first, plan.unit), (1, first, plan.unit)])
        elif kind == 1:
            per = plan.quota // CHUNK
            d, rest = divmod(b, plan.halves * per)
            h, c = divmod(rest, per)
            sources.append([(0 if h == side else 1, (d * per + c) * BLK, BLK)])
        else:
            part, row = divmod(b, plan.blocks)
            sources.append([(0 if part == side else 1, row * BLK, BLK)])
    return sources


def each_case(plan, info, kind, use):
    for a_kind in range(2):
        for a_side in range(2):

            @pl.when((kind == a_kind) & (info.side == a_side))
            def _():
                use(block_sources(plan, a_kind, a_side))


def join_blocks(plan, scalars, own, other, name):
    s = plan.s

    def body(info, own_ref, other_ref, low, high):
        def use(sources):
            for b, parts in enumerate(sources):
                out = low if b < plan.blocks else high
                row = (b % plan.blocks) * BLK
                for part, first, rows in parts:
                    src = own_ref if part == 0 else other_ref
                    out[0, row : row + rows, :] = src[0, first : first + rows, :]
                    row += rows

        each_case(plan, info, info.kind(info.side * s + pl.program_id(0)), use)

    spec = pl.BlockSpec((1, plan.tok, DH), lambda t, info: (t, 0, 0))
    return call(
        body,
        plan,
        scalars,
        (s,),
        [spec] * 2,
        [spec] * 2,
        [shape(s, plan.tok, DH)] * 2,
        "join_" + name,
        cost=copy_cost(8 * s * plan.tok * DH),
    )(own, other)


def attend(plan, scalars, wave, q_parts, k_parts, v_parts):
    koff, tok = plan.koff, plan.tok
    factor = math.log2(math.e) / math.sqrt(DH)

    def body(info, q_own, q_oth, k0, k1, k2, k3, v0, v1, v2, v3, o_own, o_oth, qs, ks, vs, os):
        kind = info.kind(info.side * plan.s + wave)
        first_block = info.pair * (2 * plan.blocks)
        vs[:, DH:] = jnp.ones((4 * tok, DH), jnp.bfloat16)
        for i, (k_ref, v_ref) in enumerate(((k0, v0), (k1, v1), (k2, v2), (k3, v3))):
            ks[i * tok : (i + 1) * tok, :] = k_ref[0]
            vs[i * tok : (i + 1) * tok, :DH] = v_ref[0]

        def load(sources):
            for b, pieces in enumerate(sources):
                row = b * BLK
                for part, first, rows in pieces:
                    src = q_own if part == 0 else q_oth
                    qs[row : row + rows, :] = src[0, first : first + rows, :]
                    row += rows

        each_case(plan, info, kind, load)

        def block(b):
            q = qs[pl.ds(pl.multiple_of(b * BLK, BLK), BLK), :]
            rows, drops = [], []
            for j in range(koff):
                goal = b + info.bands[kind * koff + j]
                ok = (first_block + goal >= 0) & (first_block + goal < plan.total)
                rows.append(pl.multiple_of((jnp.where(ok, goal, b) + plan.blocks) * BLK, BLK))
                drops.append(jnp.where(ok, 0.0, 1e30).astype(jnp.float32))
            keys = jnp.concatenate([ks[pl.ds(r, BLK), :] for r in rows], axis=0)
            scores = lax.dot_general(
                q, keys, (((1,), (1,)), ((), ())), preferred_element_type=jnp.float32
            )
            top = jnp.max(scores, axis=1, keepdims=True) * factor
            probs = jnp.concatenate(
                [
                    jnp.exp2(scores[:, j * BLK : (j + 1) * BLK] * factor - (top + drops[j])).astype(
                        jnp.bfloat16
                    )
                    for j in range(koff)
                ],
                axis=1,
            )
            vals = jnp.concatenate([vs[pl.ds(r, BLK), :] for r in rows], axis=0)
            mix = jnp.dot(probs, vals, preferred_element_type=jnp.float32)
            os[pl.ds(pl.multiple_of(b * BLK, BLK), BLK), :] = (mix[:, :DH] / mix[:, DH:]).astype(
                jnp.bfloat16
            )

        @pl.loop(0, plan.blocks)
        def _(i):
            block(2 * i)
            block(2 * i + 1)

        def store(sources):
            for b, pieces in enumerate(sources):
                row = b * BLK
                for part, first, rows in pieces:
                    dst = o_own if part == 0 else o_oth
                    dst[first : first + rows, :] = os[row : row + rows, :]
                    row += rows

        each_case(plan, info, kind, store)

    spec = pl.BlockSpec((1, tok, DH), lambda *_: (wave, 0, 0))
    pairs_count = 2 * plan.blocks * BLK * koff * BLK
    return call(
        body,
        plan,
        scalars,
        (1,),
        [spec] * 10,
        [whole(tok, DH)] * 2,
        [shape(tok, DH)] * 2,
        f"attend_{wave}",
        scratch=[
            pltpu.VMEM((2 * tok, DH), jnp.bfloat16),
            pltpu.VMEM((4 * tok, DH), jnp.bfloat16),
            pltpu.VMEM((4 * tok, 2 * DH), jnp.bfloat16),
            pltpu.VMEM((2 * tok, DH), jnp.bfloat16),
        ],
        cost=pl.CostEstimate(
            flops=4 * pairs_count * DH,
            bytes_accessed=24 * tok * DH,
            transcendentals=pairs_count,
        ),
    )(*q_parts, *k_parts, *v_parts)


def return_wave(plan, scalars, wave, own, other):
    r2 = 2 * plan.quota
    count = plan.exchanged(wave)

    def body(info, own_ref, oth_ref, *outs):
        def write(i, src):
            for p, out in enumerate(outs):
                for sp in range(plan.spans):
                    for c in range(plan.groups):
                        row = c * plan.unit + (p * plan.spans + sp) * CHUNK
                        first = sp * r2 + c * CHUNK
                        out[i, first : first + CHUNK, :] = src[row : row + CHUNK, :]

        for side in range(2):

            @pl.when(info.side == side)
            def _():
                for i in range(count):
                    write(i, own_ref if i == side else oth_ref)

    return call(
        body,
        plan,
        scalars,
        (1,),
        [whole(plan.tok, DH)] * 2,
        [whole(count, plan.piece, DH)] * plan.pairs,
        [shape(count, plan.piece, DH)] * plan.pairs,
        f"return_{wave}",
        cost=copy_cost(8 * plan.tok * DH),
    )(own, other)


def final_wave(plan, scalars, wave, pieces, own, other):
    r2 = 2 * plan.quota
    count = plan.exchanged(wave)

    def body(info, own_ref, oth_ref, *refs):
        pieces_in, out = refs[: plan.pairs], refs[plan.pairs]
        for i in range(2):
            lanes = slice(i * DH, (i + 1) * DH)
            kind = info.kind(wave + i * plan.s)

            if i < count:

                @pl.when(kind == 1)
                def _():
                    for p in range(plan.pairs):
                        for sp in range(plan.spans):
                            start = pl.multiple_of(sp * plan.span_rows + (info.pair ^ p) * r2, r2)
                            out[pl.ds(start, r2), lanes] = pieces_in[p][
                                i, sp * r2 : (sp + 1) * r2, :
                            ]

            @pl.when((kind != 1) & (info.side == i))
            def _():
                out[:, lanes] = own_ref[...]

            @pl.when((kind != 1) & (info.side != i))
            def _():
                out[:, lanes] = oth_ref[...]

    return call(
        body,
        plan,
        scalars,
        (1,),
        [whole(plan.tok, DH)] * 2 + [whole(count, plan.piece, DH)] * plan.pairs,
        whole(plan.tok, 2 * DH),
        shape(plan.tok, 2 * DH),
        f"final_{wave}",
        cost=copy_cost(12 * plan.tok * DH),
    )(own, other, *pieces)


def after(place, done):
    return lax.optimization_barrier((place, done))[0]


def hold(done, value):
    return lax.optimization_barrier((done, value))[1]


def project(plan, scalars, waves, weights):
    groups, r, _ = waves[0].shape
    _, _, _, c, d = weights[0].shape
    pairs, lots = plan.pairs, []
    for lot in weights:
        lots.append((sum(x[1] for x in lots), lot.shape[2]))

    def pair_of(m, info):
        far, shift, pair = pairs // 2, 0, info.pair
        while far:
            pair = pair ^ (((m >> shift) & 1) * far)
            far, shift = far // 2, shift + 1
        return pair

    def body(info, *refs):
        ins, ws, out, xs = refs[: len(waves)], refs[len(waves) : -2], refs[-2], refs[-1]

        @pl.when(pl.program_id(0) == 0)
        def _():
            for g in range(groups):
                for wave, x_ref in enumerate(ins):
                    for i in range(2):
                        slot = wave + i * plan.s
                        if slot < plan.hd:
                            head = info.head(slot, g)
                            xs[g * plan.hd + head] = x_ref[g, :, i * DH : (i + 1) * DH]

        def multiply(w_ref):
            total = jnp.zeros((r, 2 * d), jnp.float32)
            for g in range(groups):
                x = jnp.concatenate([xs[g * plan.hd + h] for h in range(plan.hd)], axis=1)
                w = jnp.concatenate([w_ref[y, g, 0] for y in range(2)], axis=1)
                total += jnp.dot(x, w, preferred_element_type=jnp.float32)
            out[...] = total.astype(jnp.bfloat16).reshape(out.shape)

        m = pl.program_id(0)
        for w_ref, (first, length) in zip(ws, lots):

            @pl.when((m >= first) & (m < first + length))
            def _():
                multiply(w_ref)

    aligned = 2 * d % DH == 0
    if aligned:
        out_spec = pl.BlockSpec((r, 2 * d), lambda m, info: (0, pair_of(m, info)))
        out_shape = shape(r, 2 * pairs * d)
    else:
        out_spec = pl.BlockSpec((1, r, 2 * d), lambda m, info: (pair_of(m, info), 0, 0))
        out_shape = shape(pairs, r, 2 * d)
    result = call(
        body,
        plan,
        scalars,
        (pairs,),
        [whole(groups, r, 2 * DH)] * len(waves)
        + [
            pl.BlockSpec(
                (2, groups, 1, c, d),
                lambda m, info, first=first, length=length: (
                    0,
                    0,
                    jnp.clip(m - first, 0, length - 1),
                    0,
                    0,
                ),
            )
            for first, length in lots
        ],
        out_spec,
        out_shape,
        "project",
        scratch=[pltpu.VMEM((groups * plan.hd, r, DH), jnp.bfloat16)],
        cost=pl.CostEstimate(
            flops=4 * groups * r * c * pairs * d,
            bytes_accessed=2 * (groups * r * c + 2 * pairs * groups * c * d + 2 * r * pairs * d),
            transcendentals=0,
        ),
    )(*waves, *weights)
    return result if aligned else result.transpose(1, 0, 2).reshape(r, 2 * pairs * d)


def body(queries, keys, values, w_out, head_kind, band_offsets):
    tok = queries.shape[0]
    plan = Plan(
        lax.axis_size("seq"),
        lax.axis_size("head"),
        tok,
        queries.shape[1] // DH,
        band_offsets.shape[1],
    )
    rank = lax.axis_index("seq")
    place = jnp.stack([rank >> 1, rank & 1, lax.axis_index("head")]).astype(jnp.int32)
    scalars = (place, head_kind, band_offsets.reshape(-1))
    up = [(i, i + 2) for i in range(plan.n - 2)]
    down = [(i + 2, i) for i in range(plan.n - 2)]

    order = place

    def step(run, *args):
        nonlocal order
        out = run(plan, (order, *scalars[1:]), *args)
        order = after(order, out)
        return out

    near = [
        [(2 * p + y) * plan.g + g for y in range(2) for g in range(plan.g)]
        for p in range(plan.pairs)
    ]

    def spread(lot):
        lot_all = lax.all_gather(lot, ("seq", "head"), axis=0, axis_index_groups=near)
        return lot_all.reshape(2, plan.g, *lot.shape)

    shards, far = w_out[None], plan.pairs // 2
    weights = [spread(shards)]
    coming = pair_permute(plan, shards, far)

    def more_shards():
        nonlocal shards, coming, far, order
        if far:
            arrived = hold(order, coming)
            weights.append(spread(arrived))
            far //= 2
            if far:
                shards = jnp.concatenate([shards, arrived], axis=0)
                order = after(order, shards)
                coming = pair_permute(plan, shards, far)
            else:
                order = after(order, arrived)

    def share(moved, cells, name):
        send, keep = step(share_slots, moved, cells, name)
        return keep, side_permute(plan, send)

    def extend(keep, other, name):
        low, high = step(join_blocks, keep, other, name)
        return lax.ppermute(high, "seq", up), low, high, lax.ppermute(low, "seq", down)

    moved_k = pair_exchange(plan, step(split_pieces, keys, "k"))
    moved_v = pair_exchange(plan, step(split_pieces, values, "v"))
    more_shards()
    k_parts = share(moved_k, keys, "k")
    moved_q = pair_exchange(plan, step(split_pieces, queries, "q"))
    while far:
        more_shards()
    v_parts = share(moved_v, values, "v")
    k_parts = extend(*k_parts, "k")
    q_parts = share(moved_q, queries, "q")
    v_parts = extend(*v_parts, "v")

    backs, returned, rows = [], [], []

    def attention(w):
        own, oth = step(attend, w, q_parts, k_parts, v_parts)
        backs.append((own, side_permute(plan, oth)))

    def give_back(w):
        returned.append(pair_exchange(plan, step(return_wave, w, *backs[w])))

    def finish(w):
        out = step(final_wave, w, returned[w], *backs[w])
        rows.append(
            lax.all_to_all(
                out.reshape(plan.g, tok // plan.g, 2 * DH),
                "head",
                split_axis=0,
                concat_axis=0,
                tiled=True,
            )
        )

    attention(0)
    for w in range(plan.s):
        if w + 1 < plan.s:
            attention(w + 1)
        give_back(w)
        if w:
            finish(w - 1)
    finish(plan.s - 1)
    return project(plan, scalars, rows, weights)


def solution(mesh):
    return jax.shard_map(
        body,
        mesh=mesh,
        in_specs=(P("seq", "head"), P("seq", "head"), P("seq", "head"), P("head", "seq"), P(), P()),
        out_specs=P(("seq", "head"), None),
        check_vma=False,
    )
```

time: 346 us -> 298 us (0.86)
  waiting for transfers between devices: 174 us -> 140 us
  starting transfers between devices: 80.4 us -> 61.9 us
  Pallas kernels: 45.9 us -> 58.4 us
  blocking collectives: 22.7 us -> 11.7 us
  local copies, waits for them, and re-layouts: 5.24 us -> 9.8 us
    ppermute x2, starting transfers between devices: 31 us -> 8.54 us  [extend(): lax.ppermute(high, 'seq', up)]
    ppermute x2, waiting for transfers between devices: 22.3 us -> 0.01 us  [extend(): lax.ppermute(high, 'seq', up)]
    pallas_call x12 -> x18, Pallas kernels: 45.9 us -> 58.4 us  [the longest x3 29.6 us: attend(): call(body, plan, scalars, (1,), [spec] * 10, [whole(tok, DH)] * 2, [shape...]
    ppermute x12 -> x20, waiting for transfers between devices: 122 us -> 110 us  [pair_permute(): lax.ppermute(cells, 'seq', [(2 * p + y, 2 * (p ^ k) + y) for p in range(p...]
    ppermute x4 -> x6, waiting for transfers between devices: 17.8 us -> 29.6 us  [side_permute(): return lax.ppermute(cells, 'seq', [(i, i ^ 1) for i in range(plan.n)])]
    all_to_all x1, blocking collectives: 22.7 us -> 11.7 us  [finish(): lax.all_to_all(out.reshape(plan.g, tok // plan.g, 2 * DH), 'head', split_...]
    ppermute x2, waiting for transfers between devices: 10.7 us -> 0.01 us  [extend(): lax.ppermute(low, 'seq', down)]
    all_to_all x0 -> x2, starting transfers between devices: none -> 6.94 us  [finish(): lax.all_to_all(out.reshape(plan.g, tok // plan.g, 2 * DH), 'head', split_...]
  transfers between devices with their start and end apart: 21 -> 35, of which waited for: 13 -> 13; matrix products, arithmetic and copies ran while one was open for 1% -> 1% of each run, Pallas kernels for 10% -> 15%
where the time goes in v2:
time: 298 us; the launch traced here: 297 us
  waiting for transfers between devices  140 us (47%)
  starting transfers between devices  61.9 us (21%)
  Pallas kernels  58.4 us (20%)
  between operations  13.6 us (5%)
  blocking collectives  11.7 us (4%)
  local copies, waits for them, and re-layouts  9.8 us (3%)
    ppermute x20, waiting for transfers between devices, pair_permute(): lax.ppermute(cells, 'seq', [(2 * p + y, 2 * (p ^ k) + y) for p in range(p...  110 us
    ppermute x20, starting transfers between devices, pair_permute(): lax.ppermute(cells, 'seq', [(2 * p + y, 2 * (p ^ k) + y) for p in range(p...  37 us
    ppermute x6, waiting for transfers between devices, side_permute(): return lax.ppermute(cells, 'seq', [(i, i ^ 1) for i in range(plan.n)])  29.6 us
    pallas_call x3, Pallas kernels, attend(): call(body, plan, scalars, (1,), [spec] * 10, [whole(tok, DH)] * 2, [shape...  29.6 us
    pallas_call x1, Pallas kernels, project(): call(body, plan, scalars, (pairs,), [whole(groups, r, 2 * DH)] * len(wave...  13.6 us
    all_to_all x1, blocking collectives, finish(): lax.all_to_all(out.reshape(plan.g, tok // plan.g, 2 * DH), 'head', split_...  11.7 us
    unnamed x60, local copies, waits for them, and re-layouts  9.04 us
    ppermute x2, starting transfers between devices, extend(): lax.ppermute(high, 'seq', up)  8.54 us
  transfers between devices with their start and end apart: 35, of which 13 were waited for; matrix products, arithmetic and copies ran while one was open for 1% of the time, Pallas kernels for 15%

profile of v2, /device:TPU:0, one launch (start us, length us, event | category | flops | bytes accessed | tf_op | source)
XLA Modules:
  0.0 297.4 jit_solution(1140483854759790300)
XLA Ops:
  7.3 4.1 %collective-permute-start = (bf16[1,768,384]{2,1,0:T(8,128)(2,1)}, bf16[1,768,384]{2,1,0:T(8,128)(2,1)}, u32[]{:S(2)}, u32[]{:S(2)}) collective-permute-start(bf16[1,768,384]{2,1,0:T(8,128)(2,1)} %bitcast.14), channel_id=1, source_target_pairs={{0,16},{4,20},{8,24},{12,28},{16,0},{20,4},{24,8},{28,12},{1,17},{... | collective-permute-start | bytes 1769480 | tf_op jit(solution)/shard_map/ppermute | solution.py:119
  19.6 18.1 %collective-permute-done = bf16[1,768,384]{2,1,0:T(8,128)(2,1)} collective-permute-done((bf16[1,768,384]{2,1,0:T(8,128)(2,1)}, bf16[1,768,384]{2,1,0:T(8,128)(2,1)}, u32[]{:S(2)}, u32[]{:S(2)}) %collective-permute-start) | collective-permute-done | bytes 589856 | tf_op jit(solution)/shard_map/ppermute | solution.py:119
  45.0 35.6 %collective-permute-done.1.refs_4_ = bf16[5,256,128]{2,1,0:T(8,128)(2,1)S(1)} collective-permute-done((bf16[5,256,128]{2,1,0:T(8,128)(2,1)S(1)}, bf16[5,256,128]{2,1,0:T(8,128)(2,1)S(1)}, u32[]{:S(2)}, u32[]{:S(2)}) %collective-permute-start.1) | collective-permute-done | bytes 327712 | tf_op jit(solution)/shard_map/ppermute | solution.py:119
  80.6 9.6 %collective-permute-done.3.refs_6_ = bf16[5,256,128]{2,1,0:T(8,128)(2,1)S(1)} collective-permute-done((bf16[5,256,128]{2,1,0:T(8,128)(2,1)S(1)}, bf16[5,256,128]{2,1,0:T(8,128)(2,1)S(1)}, u32[]{:S(2)}, u32[]{:S(2)}) %collective-permute-start.3) | collective-permute-done | bytes 327712 | tf_op jit(solution)/shard_map/ppermute | solution.py:119
  102.0 9.4 %collective-permute-done.5.refs_4_ = bf16[5,256,128]{2,1,0:T(8,128)(2,1)S(1)} collective-permute-done((bf16[5,256,128]{2,1,0:T(8,128)(2,1)}, bf16[5,256,128]{2,1,0:T(8,128)(2,1)S(1)}, u32[]{:S(2)}, u32[]{:S(2)}) %collective-permute-start.5) | collective-permute-done | bytes 327712 | tf_op jit(solution)/shard_map/ppermute | solution.py:119
  111.4 10.6 %collective-permute-done.6.refs_5_ = bf16[5,256,128]{2,1,0:T(8,128)(2,1)S(1)} collective-permute-done((bf16[5,256,128]{2,1,0:T(8,128)(2,1)}, bf16[5,256,128]{2,1,0:T(8,128)(2,1)S(1)}, u32[]{:S(2)}, u32[]{:S(2)}) %collective-permute-start.6) | collective-permute-done | bytes 327712 | tf_op jit(solution)/shard_map/ppermute | solution.py:119
  125.0 6.0 %collective-permute-start.10 = (bf16[5,256,128]{2,1,0:T(8,128)(2,1)}, bf16[5,256,128]{2,1,0:T(8,128)(2,1)S(1)}, u32[]{:S(2)}, u32[]{:S(2)}) collective-permute-start(bf16[5,256,128]{2,1,0:T(8,128)(2,1)} %copy-done.22), channel_id=1, source_target_pairs={{0,16},{4,20},{8,24},{12,28},{16,0},{20,4},{24,8},{28,12},{1,17},{... | collective-permute-start | bytes 983048 | tf_op jit(solution)/shard_map/ppermute | solution.py:119
  131.0 2.4 collective-permute-start.11
  134.4 3.8 %collective-permute-start.14 = (bf16[3,1024,128]{2,1,0:T(8,128)(2,1)S(1)}, bf16[3,1024,128]{2,1,0:T(8,128)(2,1)S(1)}, u32[]{:S(2)}, u32[]{:S(2)}) collective-permute-start(bf16[3,1024,128]{2,1,0:T(8,128)(2,1)S(1)} %get-tuple-element.91.refs_7_), channel_id=1, source_target_pairs={{0,8},{4,12},{8,16},{12,20},{16,24},{20,28},{1,9},{5,13},{9,17},{1... | collective-permute-start | bytes 2359304 | tf_op jit(solution)/shard_map/ppermute | solution.py:574
  138.3 15.7 %collective-permute-done.10.refs_5_ = bf16[5,256,128]{2,1,0:T(8,128)(2,1)S(1)} collective-permute-done((bf16[5,256,128]{2,1,0:T(8,128)(2,1)}, bf16[5,256,128]{2,1,0:T(8,128)(2,1)S(1)}, u32[]{:S(2)}, u32[]{:S(2)}) %collective-permute-start.10) | collective-permute-done | bytes 327712 | tf_op jit(solution)/shard_map/ppermute | solution.py:119
  157.4 3.5 %collective-permute-done.12.refs_4_ = bf16[3,1024,128]{2,1,0:T(8,128)(2,1)S(1)} collective-permute-done((bf16[3,1024,128]{2,1,0:T(8,128)(2,1)S(1)}, bf16[3,1024,128]{2,1,0:T(8,128)(2,1)S(1)}, u32[]{:S(2)}, u32[]{:S(2)}) %collective-permute-start.12) | collective-permute-done | bytes 786464 | tf_op jit(solution)/shard_map/ppermute | solution.py:115
  161.7 4.7 %collective-permute-start.16 = (bf16[3,1024,128]{2,1,0:T(8,128)(2,1)S(1)}, bf16[3,1024,128]{2,1,0:T(8,128)(2,1)S(1)}, u32[]{:S(2)}, u32[]{:S(2)}) collective-permute-start(bf16[3,1024,128]{2,1,0:T(8,128)(2,1)S(1)} %get-tuple-element.97.refs_11_), channel_id=1, source_target_pairs={{0,8},{4,12},{8,16},{12,20},{16,24},{20,28},{1,9},{5,13},{9,17},{1... | collective-permute-start | bytes 2359304 | tf_op jit(solution)/shard_map/ppermute | solution.py:574
  167.7 22.5 %collective-permute-done.13.refs_4_ = bf16[3,1024,128]{2,1,0:T(8,128)(2,1)S(1)} collective-permute-done((bf16[3,1024,128]{2,1,0:T(8,128)(2,1)S(1)}, bf16[3,1024,128]{2,1,0:T(8,128)(2,1)S(1)}, u32[]{:S(2)}, u32[]{:S(2)}) %collective-permute-start.13) | collective-permute-done | bytes 786464 | tf_op jit(solution)/shard_map/ppermute | solution.py:115
  191.2 9.9 %attend_0.1 = (bf16[1024,128]{1,0:T(8,128)(2,1)S(1)}, bf16[1024,128]{1,0:T(8,128)(2,1)S(1)}) custom-call(s32[3]{0:T(128)S(1)} %pad_add_fusion.refs_0_, s32[24]{0:T(128)S(1)} %copy-done.12, s32[14]{0:T(128)S(1)} %reshape.21.refs_2_, bf16[3,1024,128]{2,1,0:T(8,128)(2,1)S(1)} %get-tuple-element.94.refs_3_, ...), custom_call_target="tpu_custom_call" | custom-call | flops 1879048192 | bytes 3145728 | tf_op jit(solution)/shard_map/attend_0/pallas_call | solution.py:332
  202.6 9.9 %attend_1.1 = (bf16[1024,128]{1,0:T(8,128)(2,1)S(1)}, bf16[1024,128]{1,0:T(8,128)(2,1)S(1)}) custom-call(s32[3]{0:T(128)S(1)} %pad_add_fusion.refs_0_, s32[24]{0:T(128)S(1)} %copy-done.12, s32[14]{0:T(128)S(1)} %reshape.21.refs_2_, bf16[3,1024,128]{2,1,0:T(8,128)(2,1)S(1)} %get-tuple-element.94.refs_3_, ...), custom_call_target="tpu_custom_call" | custom-call | flops 1879048192 | bytes 3145728 | tf_op jit(solution)/shard_map/attend_1/pallas_call | solution.py:332
  218.8 9.9 %attend_2.1 = (bf16[1024,128]{1,0:T(8,128)(2,1)S(1)}, bf16[1024,128]{1,0:T(8,128)(2,1)S(1)}) custom-call(s32[3]{0:T(128)S(1)} %pad_add_fusion.refs_0_, s32[24]{0:T(128)S(1)} %copy-done.12, s32[14]{0:T(128)S(1)} %reshape.21.refs_2_, bf16[3,1024,128]{2,1,0:T(8,128)(2,1)S(1)} %get-tuple-element.94.refs_3_, ...), custom_call_target="tpu_custom_call" | custom-call | flops 1879048192 | bytes 3145728 | tf_op jit(solution)/shard_map/attend_2/pallas_call | solution.py:332
  231.0 3.5 %all-to-all-start = ((bf16[4,256,256]{2,1,0:T(8,128)(2,1)}), bf16[4,256,256]{2,1,0:T(8,128)(2,1)S(1)}, u32[]{:S(2)}, u32[]{:S(2)}) async-start(bf16[4,256,256]{2,1,0:T(8,128)(2,1)} %bitcast.4), calls=%async_computation | async-start | bytes 1048576 | tf_op jit(solution)/shard_map/all_to_all | solution.py:600
  239.8 3.5 %collective-permute-done.23.refs_4_ = bf16[1024,128]{1,0:T(8,128)(2,1)S(1)} collective-permute-done((bf16[1024,128]{1,0:T(8,128)(2,1)S(1)}, bf16[1024,128]{1,0:T(8,128)(2,1)S(1)}, u32[]{:S(2)}, u32[]{:S(2)}) %collective-permute-start.23) | collective-permute-done | bytes 262176 | tf_op jit(solution)/shard_map/ppermute | solution.py:115
  243.8 5.2 %collective-permute-done.25.refs_7_ = bf16[2,256,128]{2,1,0:T(8,128)(2,1)S(1)} collective-permute-done((bf16[2,256,128]{2,1,0:T(8,128)(2,1)S(1)}, bf16[2,256,128]{2,1,0:T(8,128)(2,1)S(1)}, u32[]{:S(2)}, u32[]{:S(2)}) %collective-permute-start.25) | collective-permute-done | bytes 131104 | tf_op jit(solution)/shard_map/ppermute | solution.py:119
  250.6 3.5 %all-to-all-start.1 = ((bf16[4,256,256]{2,1,0:T(8,128)(2,1)}), bf16[4,256,256]{2,1,0:T(8,128)(2,1)S(1)}, u32[]{:S(2)}, u32[]{:S(2)}) async-start(bf16[4,256,256]{2,1,0:T(8,128)(2,1)} %bitcast.5), calls=%async_computation.1 | async-start | bytes 1048576 | tf_op jit(solution)/shard_map/all_to_all | solution.py:600
  254.1 2.4 collective-permute-start.27
  259.1 5.7 %collective-permute-done.28.refs_7_ = bf16[1,256,128]{2,1,0:T(8,128)(2,1)S(1)} collective-permute-done((bf16[1,256,128]{2,1,0:T(8,128)(2,1)S(1)}, bf16[1,256,128]{2,1,0:T(8,128)(2,1)S(1)}, u32[]{:S(2)}, u32[]{:S(2)}) %collective-permute-start.28) | collective-permute-done | bytes 65568 | tf_op jit(solution)/shard_map/ppermute | solution.py:119
  265.6 11.7 %all_to_all.15.refs_5_ = bf16[4,256,256]{2,1,0:T(8,128)(2,1)S(1)} all-to-all(bf16[4,256,256]{2,1,0:T(8,128)(2,1)S(1)} %bitcast.10), channel_id=1, replica_groups=mesh['seq'=8,'head'=4] {'head'}, dimensions={0} | all-to-all | bytes 1048576 | tf_op jit(solution)/shard_map/all_to_all | solution.py:600
  277.2 13.6 %project.1 = bf16[256,3072]{1,0:T(8,128)(2,1)} custom-call(s32[3]{0:T(128)S(1)} %pad_add_fusion.refs_0_, s32[24]{0:T(128)S(1)} %copy-done.12, s32[14]{0:T(128)S(1)} %reshape.21.refs_2_, bf16[4,256,256]{2,1,0:T(8,128)(2,1)S(1)} %all-to-all-done.refs_3_, bf16[4,256,256]{2,1,0:T(8,128)(2,1)S(1)} %all-to-all-done.1.refs_4_, ...), custom_call_target="tpu_custom_call" | custom-call | flops 4831838208 | bytes 22020096 | tf_op jit(solution)/shard_map/project/pallas_call | solution.py:487
  (131 shorter events, 59.2 us)
Async XLA Ops:
  6.5 270.7 %all-gather.7.cloned.1.call-start = ((), (), s32[]{:S(2)}) async-start(), calls=%async_computation.3 | async-start | bytes 5308416 | tf_op jit(solution)/shard_map/all_gather | solution.py:548
  7.3 270.0 %all-gather.9.cloned.1.call-start = ((), (), s32[]{:S(2)}) async-start(), calls=%async_computation.4 | async-start | bytes 5308416 | tf_op jit(solution)/shard_map/all_gather | solution.py:548
  7.3 30.4 %collective-permute-start = (bf16[1,768,384]{2,1,0:T(8,128)(2,1)}, bf16[1,768,384]{2,1,0:T(8,128)(2,1)}, u32[]{:S(2)}, u32[]{:S(2)}) collective-permute-start(bf16[1,768,384]{2,1,0:T(8,128)(2,1)} %bitcast.14), channel_id=1, source_target_pairs={{0,16},{4,20},{8,24},{12,28},{16,0},{20,4},{24,8},{28,12},{1,17},{... | collective-permute-start | bytes 1769480 | tf_op jit(solution)/shard_map/ppermute | solution.py:119
  37.7 239.5 %all-gather.11.cloned.1.call-start = ((), (), s32[]{:S(2)}) async-start(), calls=%async_computation.5 | async-start | bytes 10616832 | tf_op jit(solution)/shard_map/all_gather | solution.py:548
  39.3 56.7 %collective-permute-start.4 = (bf16[2,768,384]{2,1,0:T(8,128)(2,1)S(1)}, bf16[2,768,384]{2,1,0:T(8,128)(2,1)}, u32[]{:S(2)}, u32[]{:S(2)}) collective-permute-start(bf16[2,768,384]{2,1,0:T(8,128)(2,1)S(1)} %pad_maximum_fusion), channel_id=1, source_target_pairs={{0,8},{4,12},{8,0},{12,4},{16,24},{20,28},{24,16},{28,20},{1,9},{5... | collective-permute-start | bytes 3538952 | tf_op jit(solution)/shard_map/ppermute | solution.py:119
  40.1 40.5 %collective-permute-start.1 = (bf16[5,256,128]{2,1,0:T(8,128)(2,1)S(1)}, bf16[5,256,128]{2,1,0:T(8,128)(2,1)S(1)}, u32[]{:S(2)}, u32[]{:S(2)}) collective-permute-start(bf16[5,256,128]{2,1,0:T(8,128)(2,1)S(1)} %copy-done.28), channel_id=1, source_target_pairs={{0,8},{4,12},{8,0},{12,4},{16,24},{20,28},{24,16},{28,20},{1,9},{5... | collective-permute-start | bytes 983048 | tf_op jit(solution)/shard_map/ppermute | solution.py:119
  41.4 39.2 %collective-permute-start.2 = (bf16[5,256,128]{2,1,0:T(8,128)(2,1)S(1)}, bf16[5,256,128]{2,1,0:T(8,128)(2,1)S(1)}, u32[]{:S(2)}, u32[]{:S(2)}) collective-permute-start(bf16[5,256,128]{2,1,0:T(8,128)(2,1)S(1)} %copy-done.26), channel_id=1, source_target_pairs={{0,16},{4,20},{8,24},{12,28},{16,0},{20,4},{24,8},{28,12},{1,17},{... | collective-permute-start | bytes 983048 | tf_op jit(solution)/shard_map/ppermute | solution.py:119
  43.6 46.6 %collective-permute-start.3 = (bf16[5,256,128]{2,1,0:T(8,128)(2,1)S(1)}, bf16[5,256,128]{2,1,0:T(8,128)(2,1)S(1)}, u32[]{:S(2)}, u32[]{:S(2)}) collective-permute-start(bf16[5,256,128]{2,1,0:T(8,128)(2,1)S(1)} %copy-done.24), channel_id=1, source_target_pairs={{0,24},{4,28},{8,16},{12,20},{16,8},{20,12},{24,0},{28,4},{1,25},{... | collective-permute-start | bytes 983048 | tf_op jit(solution)/shard_map/ppermute | solution.py:119
  96.0 15.4 %collective-permute-start.5 = (bf16[5,256,128]{2,1,0:T(8,128)(2,1)}, bf16[5,256,128]{2,1,0:T(8,128)(2,1)S(1)}, u32[]{:S(2)}, u32[]{:S(2)}) collective-permute-start(bf16[5,256,128]{2,1,0:T(8,128)(2,1)} %copy-done.21), channel_id=1, source_target_pairs={{0,8},{4,12},{8,0},{12,4},{16,24},{20,28},{24,16},{28,20},{1,9},{5... | collective-permute-start | bytes 983048 | tf_op jit(solution)/shard_map/ppermute | solution.py:119
  96.1 25.9 %collective-permute-start.6 = (bf16[5,256,128]{2,1,0:T(8,128)(2,1)}, bf16[5,256,128]{2,1,0:T(8,128)(2,1)S(1)}, u32[]{:S(2)}, u32[]{:S(2)}) collective-permute-start(bf16[5,256,128]{2,1,0:T(8,128)(2,1)} %copy-done.19), channel_id=1, source_target_pairs={{0,16},{4,20},{8,24},{12,28},{16,0},{20,4},{24,8},{28,12},{1,17},{... | collective-permute-start | bytes 983048 | tf_op jit(solution)/shard_map/ppermute | solution.py:119
  98.4 23.6 %collective-permute-start.7 = (bf16[5,256,128]{2,1,0:T(8,128)(2,1)S(1)}, bf16[5,256,128]{2,1,0:T(8,128)(2,1)S(1)}, u32[]{:S(2)}, u32[]{:S(2)}) collective-permute-start(bf16[5,256,128]{2,1,0:T(8,128)(2,1)S(1)} %copy-done.16), channel_id=1, source_target_pairs={{0,24},{4,28},{8,16},{12,20},{16,8},{20,12},{24,0},{28,4},{1,25},{... | collective-permute-start | bytes 983048 | tf_op jit(solution)/shard_map/ppermute | solution.py:119
  100.5 33.1 %collective-permute-start.8 = (bf16[3,1024,128]{2,1,0:T(8,128)(2,1)S(1)}, bf16[3,1024,128]{2,1,0:T(8,128)(2,1)S(1)}, u32[]{:S(2)}, u32[]{:S(2)}) collective-permute-start(bf16[3,1024,128]{2,1,0:T(8,128)(2,1)S(1)} %copy-done.14), channel_id=1, source_target_pairs={{0,4},{4,0},{8,12},{12,8},{16,20},{20,16},{24,28},{28,24},{1,5},{5... | collective-permute-start | bytes 2359304 | tf_op jit(solution)/shard_map/ppermute | solution.py:115
  123.4 37.5 %collective-permute-start.12 = (bf16[3,1024,128]{2,1,0:T(8,128)(2,1)S(1)}, bf16[3,1024,128]{2,1,0:T(8,128)(2,1)S(1)}, u32[]{:S(2)}, u32[]{:S(2)}) collective-permute-start(bf16[3,1024,128]{2,1,0:T(8,128)(2,1)S(1)} %get-tuple-element.87), channel_id=1, source_target_pairs={{0,4},{4,0},{8,12},{12,8},{16,20},{20,16},{24,28},{28,24},{1,5},{5... | collective-permute-start | bytes 2359304 | tf_op jit(solution)/shard_map/ppermute | solution.py:115
  125.0 28.9 %collective-permute-start.10 = (bf16[5,256,128]{2,1,0:T(8,128)(2,1)}, bf16[5,256,128]{2,1,0:T(8,128)(2,1)S(1)}, u32[]{:S(2)}, u32[]{:S(2)}) collective-permute-start(bf16[5,256,128]{2,1,0:T(8,128)(2,1)} %copy-done.22), channel_id=1, source_target_pairs={{0,16},{4,20},{8,24},{12,28},{16,0},{20,4},{24,8},{28,12},{1,17},{... | collective-permute-start | bytes 983048 | tf_op jit(solution)/shard_map/ppermute | solution.py:119
  131.0 24.2 %collective-permute-start.11 = (bf16[5,256,128]{2,1,0:T(8,128)(2,1)}, bf16[5,256,128]{2,1,0:T(8,128)(2,1)S(1)}, u32[]{:S(2)}, u32[]{:S(2)}) collective-permute-start(bf16[5,256,128]{2,1,0:T(8,128)(2,1)} %copy-done.20), channel_id=1, source_target_pairs={{0,24},{4,28},{8,16},{12,20},{16,8},{20,12},{24,0},{28,4},{1,25},{... | collective-permute-start | bytes 983048 | tf_op jit(solution)/shard_map/ppermute | solution.py:119
  133.4 21.8 %collective-permute-start.9 = (bf16[5,256,128]{2,1,0:T(8,128)(2,1)S(1)}, bf16[5,256,128]{2,1,0:T(8,128)(2,1)S(1)}, u32[]{:S(2)}, u32[]{:S(2)}) collective-permute-start(bf16[5,256,128]{2,1,0:T(8,128)(2,1)S(1)} %copy-done.18), channel_id=1, source_target_pairs={{0,8},{4,12},{8,0},{12,4},{16,24},{20,28},{24,16},{28,20},{1,9},{5... | collective-permute-start | bytes 983048 | tf_op jit(solution)/shard_map/ppermute | solution.py:119
  134.4 55.8 %collective-permute-start.14 = (bf16[3,1024,128]{2,1,0:T(8,128)(2,1)S(1)}, bf16[3,1024,128]{2,1,0:T(8,128)(2,1)S(1)}, u32[]{:S(2)}, u32[]{:S(2)}) collective-permute-start(bf16[3,1024,128]{2,1,0:T(8,128)(2,1)S(1)} %get-tuple-element.91.refs_7_), channel_id=1, source_target_pairs={{0,8},{4,12},{8,16},{12,20},{16,24},{20,28},{1,9},{5,13},{9,17},{1... | collective-permute-start | bytes 2359304 | tf_op jit(solution)/shard_map/ppermute | solution.py:574
  153.9 36.3 %collective-permute-start.15 = (bf16[3,1024,128]{2,1,0:T(8,128)(2,1)S(1)}, bf16[3,1024,128]{2,1,0:T(8,128)(2,1)S(1)}, u32[]{:S(2)}, u32[]{:S(2)}) collective-permute-start(bf16[3,1024,128]{2,1,0:T(8,128)(2,1)S(1)} %get-tuple-element.90.refs_6_), channel_id=1, source_target_pairs={{8,0},{12,4},{16,8},{20,12},{24,16},{28,20},{9,1},{13,5},{17,9},{2... | collective-permute-start | bytes 2359304 | tf_op jit(solution)/shard_map/ppermute | solution.py:574
  156.7 33.5 %collective-permute-start.13 = (bf16[3,1024,128]{2,1,0:T(8,128)(2,1)S(1)}, bf16[3,1024,128]{2,1,0:T(8,128)(2,1)S(1)}, u32[]{:S(2)}, u32[]{:S(2)}) collective-permute-start(bf16[3,1024,128]{2,1,0:T(8,128)(2,1)S(1)} %get-tuple-element.93), channel_id=1, source_target_pairs={{0,4},{4,0},{8,12},{12,8},{16,20},{20,16},{24,28},{28,24},{1,5},{5... | collective-permute-start | bytes 2359304 | tf_op jit(solution)/shard_map/ppermute | solution.py:115
  161.7 28.5 %collective-permute-start.16 = (bf16[3,1024,128]{2,1,0:T(8,128)(2,1)S(1)}, bf16[3,1024,128]{2,1,0:T(8,128)(2,1)S(1)}, u32[]{:S(2)}, u32[]{:S(2)}) collective-permute-start(bf16[3,1024,128]{2,1,0:T(8,128)(2,1)S(1)} %get-tuple-element.97.refs_11_), channel_id=1, source_target_pairs={{0,8},{4,12},{8,16},{12,20},{16,24},{20,28},{1,9},{5,13},{9,17},{1... | collective-permute-start | bytes 2359304 | tf_op jit(solution)/shard_map/ppermute | solution.py:574
  166.4 23.8 %collective-permute-start.17 = (bf16[3,1024,128]{2,1,0:T(8,128)(2,1)S(1)}, bf16[3,1024,128]{2,1,0:T(8,128)(2,1)S(1)}, u32[]{:S(2)}, u32[]{:S(2)}) collective-permute-start(bf16[3,1024,128]{2,1,0:T(8,128)(2,1)S(1)} %get-tuple-element.96.refs_10_), channel_id=1, source_target_pairs={{8,0},{12,4},{16,8},{20,12},{24,16},{28,20},{9,1},{13,5},{17,9},{2... | collective-permute-start | bytes 2359304 | tf_op jit(solution)/shard_map/ppermute | solution.py:574
  212.5 16.3 %collective-permute-start.19 = (bf16[1024,128]{1,0:T(8,128)(2,1)S(1)}, bf16[1024,128]{1,0:T(8,128)(2,1)S(1)}, u32[]{:S(2)}, u32[]{:S(2)}) collective-permute-start(bf16[1024,128]{1,0:T(8,128)(2,1)S(1)} %get-tuple-element.103), channel_id=1, source_target_pairs={{0,4},{4,0},{8,12},{12,8},{16,20},{20,16},{24,28},{28,24},{1,5},{5... | collective-permute-start | bytes 786440 | tf_op jit(solution)/shard_map/ppermute | solution.py:115
  213.7 15.6 %collective-permute-start.20 = (bf16[2,256,128]{2,1,0:T(8,128)(2,1)S(1)}, bf16[2,256,128]{2,1,0:T(8,128)(2,1)S(1)}, u32[]{:S(2)}, u32[]{:S(2)}) collective-permute-start(bf16[2,256,128]{2,1,0:T(8,128)(2,1)S(1)} %get-tuple-element.106), channel_id=1, source_target_pairs={{0,8},{4,12},{8,0},{12,4},{16,24},{20,28},{24,16},{28,20},{1,9},{5... | collective-permute-start | bytes 393224 | tf_op jit(solution)/shard_map/ppermute | solution.py:119
  231.0 19.6 %all-to-all-start = ((bf16[4,256,256]{2,1,0:T(8,128)(2,1)}), bf16[4,256,256]{2,1,0:T(8,128)(2,1)S(1)}, u32[]{:S(2)}, u32[]{:S(2)}) async-start(bf16[4,256,256]{2,1,0:T(8,128)(2,1)} %bitcast.4), calls=%async_computation | async-start | bytes 1048576 | tf_op jit(solution)/shard_map/all_to_all | solution.py:600
  (41 other events, 597.7 us)
Sparse Core Ops, SparseCore 0:
  9.2 41.6 all-gather.6
  52.8 38.9 all-gather.8
  96.1 95.0 all-gather.10
